TPU v7x, 32 devices: a whole 2x2x4 slice. The times are simulated.
32 devices in a mesh: row: 4 (over z), ma: 8 (over y, x, core).
Axes of the slice: x: 2, y: 2, z: 4, core: 2. Of those that a mesh axis runs over, the one named last changes fastest.
Arguments:
- spectra: float32 [4, 2, 128, 4224], P(None, None, 'row', 'ma'), may hold values from -6 to 6
- dtheta_table: bfloat16 [4224, 768], P('ma'), may hold values from -0.046875 to 0.046875
- dphi_table: bfloat16 [4224, 768], P('ma'), may hold values from -0.046875 to 0.046875
- analysis_table: bfloat16 [4224, 768], P('ma'), may hold values from -6 to 6
- pair_index: int32 [8], replicated, may hold values from 0 to 255, as said below
- diffusivity: float32 [4], replicated, may hold values from 0.0001 to 0.0004
Outputs:
- new_spectra: float32 [4, 2, 128, 4224], P(None, None, 'row', 'ma')
Inputs may be any that keep to these rules, and one draw needn't show every extreme that they name: 8 distinct values, among them always both 0 and the largest; position g holds the orders pair_index[g] and 511 - pair_index[g].
All inputs are finite; a program needn't handle non-finite values.
Results may differ from a plain program's by a relative error of at most 0.0057.
Values may be sent and summed in bfloat16 or wider, within the bound.
A program may use at most 64 MiB of HBM per device.

v0:
```python
import math

import jax
import jax.numpy as jnp
from jax import lax
from jax.sharding import PartitionSpec as P

LMAX = 511
NPHI = 1536
SLOTS = 528


ROTATION = 2.0
SHELL_RADIUS = 16.0


def slot_layout(pair_values):
    slot_index = jnp.arange(SLOTS, dtype=jnp.int32)[None, :]
    lowest = pair_values[:, None]
    first_part = slot_index < LMAX + 1 - lowest
    second_part = jnp.logical_and(jnp.logical_not(first_part), slot_index < LMAX + 2)
    degree = jnp.where(first_part, lowest + slot_index, slot_index - 1)
    wave_order = jnp.where(first_part, lowest, LMAX - lowest)
    return (first_part, second_part, degree, wave_order)


def fourier_tables(pair_values):
    orders = jnp.stack([pair_values, LMAX - pair_values], axis=1)
    angle_step = jnp.arange(NPHI, dtype=jnp.int32)
    phases = orders[:, :, None] * angle_step[None, None, :] % NPHI
    angles = phases.astype(jnp.float32) * (2.0 * math.pi / NPHI)
    weight_order = jnp.where(orders == 0, 1.0, 2.0).astype(jnp.float32)[:, :, None]
    cosine = jnp.cos(angles)
    sine_part = jnp.sin(angles)
    synthesis = jnp.stack([weight_order * cosine, -weight_order * sine_part]).astype(jnp.bfloat16)
    analysis_fourier = (jnp.stack([cosine, -sine_part]) / NPHI).astype(jnp.bfloat16)
    return (synthesis, analysis_fourier)


def grid_products(grid_values):
    stream_theta, stream_phi, poloidal_theta, poloidal_phi = (
        grid_values[0],
        grid_values[1],
        grid_values[2],
        grid_values[3],
    )
    thermal_theta, thermal_phi, magnetic_theta, magnetic_phi = (
        grid_values[4],
        grid_values[5],
        grid_values[6],
        grid_values[7],
    )
    flow_theta = poloidal_theta - stream_phi
    flow_phi = poloidal_phi + stream_theta
    field_theta = -magnetic_phi
    stress = field_theta * magnetic_theta - flow_theta * flow_phi
    pressure = 0.5 * (magnetic_theta * magnetic_theta - field_theta * field_theta) - 0.5 * (
        flow_phi * flow_phi - flow_theta * flow_theta
    )
    heat_flux = -(flow_theta * thermal_theta + flow_phi * thermal_phi)
    induction = -(flow_theta * magnetic_theta - flow_phi * field_theta)
    return jnp.stack([stress, pressure, heat_flux, induction])


def coupled(source, partner, parity, degree, wave_order, alive):
    degree_real = degree.astype(jnp.float32)
    order_real = wave_order.astype(jnp.float32)
    lower_coupling = jnp.sqrt(
        (degree_real * degree_real - order_real * order_real)
        * alive
        / jnp.maximum(4.0 * degree_real * degree_real - 1.0, 1.0)
    )
    upper_degree = degree_real + 1.0
    upper_coupling = (
        jnp.sqrt(
            (upper_degree * upper_degree - order_real * order_real)
            / (4.0 * upper_degree * upper_degree - 1.0)
        )
        * alive
        * (degree < LMAX).astype(jnp.float32)
    )
    spin_term = order_real / (degree_real * (degree_real + 1.0) + 2.0)
    turned = jnp.stack([-source[1], source[0]])
    below_slot = jnp.concatenate([jnp.zeros_like(partner[..., :1]), partner[..., :-1]], axis=-1)
    above_slot = jnp.concatenate([partner[..., 1:], jnp.zeros_like(partner[..., :1])], axis=-1)
    return ROTATION * (
        spin_term * turned + parity * (lower_coupling * below_slot + upper_coupling * above_slot)
    )


def radial_solve(right_side, degree_flat, diffusivity):
    points = right_side.shape[2]
    counter = jnp.arange(1, points + 1, dtype=jnp.int32)
    product = counter[:, None] * counter[None, :] % (2 * (points + 1))
    sine_basis = math.sqrt(2.0 / (points + 1)) * jnp.sin(
        product.astype(jnp.float32) * (math.pi / (points + 1))
    )
    eigenvalues = (
        4.0
        * (points + 1)
        * (points + 1)
        * jnp.sin(counter.astype(jnp.float32) * (math.pi / (2 * (points + 1)))) ** 2
    )
    degree_real = degree_flat.astype(jnp.float32)
    horizontal = degree_real * (degree_real + 1.0) / (SHELL_RADIUS * SHELL_RADIUS)
    modal_part = jnp.einsum(
        "jk,fcks->fcjs", sine_basis, right_side, precision=lax.Precision.HIGHEST
    )
    factor = 1.0 + diffusivity[:, None, None, None] * (
        eigenvalues[None, None, :, None] + horizontal[None, None, None, :]
    )
    return jnp.einsum(
        "jk,fcks->fcjs", sine_basis, modal_part / factor, precision=lax.Precision.HIGHEST
    )


def local(spectra, dtheta_table, dphi_table, analysis_table, pair_index, diffusivity):
    local_pairs = spectra.shape[3] // SLOTS
    radius_count = spectra.shape[2]
    theta_count = dtheta_table.shape[1]
    columns = local_pairs * SLOTS
    own_pairs = lax.dynamic_slice_in_dim(
        pair_index, lax.axis_index("ma") * local_pairs, local_pairs
    )
    first_part, second_part, degree, wave_order = slot_layout(own_pairs)
    alive = jnp.logical_or(first_part, second_part).astype(jnp.float32)
    part_masks = jnp.stack([first_part, second_part], axis=1).astype(jnp.float32)
    masked_state = spectra.reshape(4, 2, radius_count, local_pairs, SLOTS) * alive
    coeffs = masked_state.astype(jnp.bfloat16)
    spread = coeffs[:, :, :, :, None, :] * part_masks.astype(jnp.bfloat16)[None, None, None]
    theta_rows = dtheta_table.reshape(local_pairs, SLOTS, theta_count)
    phi_rows = dphi_table.reshape(local_pairs, SLOTS, theta_count)
    along_theta = jnp.einsum(
        "fcrpjs,pst->fcrpjt", spread, theta_rows, preferred_element_type=jnp.float32
    )
    phi_direct = jnp.einsum(
        "fcrpjs,pst->fcrpjt", spread, phi_rows, preferred_element_type=jnp.float32
    )
    along_phi = jnp.stack([-phi_direct[:, 1], phi_direct[:, 0]], axis=1)
    grid_spectra = jnp.stack([along_theta, along_phi], axis=1)
    grid_spectra = (
        jnp.transpose(grid_spectra, (3, 0, 1, 2, 4, 5, 6))
        .reshape(radius_count, 8, 2, local_pairs, 2, theta_count)
        .astype(jnp.bfloat16)
    )
    synthesis, analysis_fourier = fourier_tables(pair_index)

    def one_radius(radius_block):
        grid_values = jnp.einsum(
            "qcpjt,cpjk->qtk", radius_block, synthesis, preferred_element_type=jnp.float32
        )
        products = grid_products(grid_values).astype(jnp.bfloat16)
        return jnp.einsum(
            "ftk,cpjk->fcpjt", products, analysis_fourier, preferred_element_type=jnp.float32
        ).astype(jnp.bfloat16)

    latitudes = lax.all_to_all(grid_spectra, "ma", split_axis=5, concat_axis=3, tiled=True)
    computed = lax.map(one_radius, latitudes)
    returned = lax.all_to_all(computed, "ma", split_axis=3, concat_axis=5, tiled=True)
    analysis_rows = analysis_table.reshape(local_pairs, SLOTS, theta_count)
    projected = jnp.einsum(
        "rfcpjt,pst->fcrpjs", returned, analysis_rows, preferred_element_type=jnp.float32
    )
    nonlinear = jnp.sum(projected * part_masks[None, None, None], axis=4)
    forcing = jnp.stack(
        [
            coupled(masked_state[0], masked_state[1], 1.0, degree, wave_order, alive),
            coupled(masked_state[1], masked_state[0], -1.0, degree, wave_order, alive),
        ]
    )
    forcing = jnp.concatenate([forcing, jnp.zeros_like(forcing)], axis=0)
    right_side = (masked_state + nonlinear + forcing) * alive
    pencils = lax.all_to_all(
        right_side.reshape(4, 2, radius_count, columns),
        "row",
        split_axis=3,
        concat_axis=2,
        tiled=True,
    )
    share_size = columns // lax.axis_size("row")
    degree_share = lax.dynamic_slice_in_dim(
        degree.reshape(columns), lax.axis_index("row") * share_size, share_size
    )
    solved = radial_solve(pencils, degree_share, diffusivity)
    shells = lax.all_to_all(solved, "row", split_axis=2, concat_axis=3, tiled=True)
    return shells * alive.reshape(columns)


def solution(mesh):
    return jax.shard_map(
        local,
        mesh=mesh,
        in_specs=(
            P(None, None, "row", "ma"),
            P("ma", None),
            P("ma", None),
            P("ma", None),
            P(),
            P(),
        ),
        out_specs=P(None, None, "row", "ma"),
        check_vma=False,
    )
```

profile of v0, /device:TPU:0, one launch (start us, length us, event | category | flops | bytes accessed | tf_op | source)
XLA Modules:
  0.0 245.4 jit_solution(5899633462003070407)
XLA Ops:
  0.0 1.4 dynamic_slice.10
  3.3 1.2 fusion.98
  5.4 1.0 copy-done.16
  7.6 11.3 %copy.34 = bf16[32,8,2,1,2,768]{0,4,2,1,3,5:T(2,128)(2,1)} copy(bf16[32,8,2,1,2,768]{5,0,4,2,1,3:T(8,128)(2,1)S(1)} %bitcast.167) | data formatting | bytes 3145728 | tf_op jit(solution)/shard_map/convert_element_type | solution.py:144
  18.9 9.5 %reshape.518 = bf16[8,2,49152]{2,1,0:T(2,128)(2,1)} reshape(bf16[768,1,8,2,2,32]{5,4,3,2,1,0:T(2,128)(2,1)} %bitcast.163) | data formatting | bytes 3145728
  28.4 5.3 %all-to-all-start = ((bf16[8,2,49152]{2,1,0:T(2,128)(2,1)}), bf16[8,2,49152]{2,1,0:T(2,128)(2,1)S(1)}, u32[]{:S(2)}, u32[]{:S(2)}) async-start(bf16[8,2,49152]{2,1,0:T(2,128)(2,1)} %reshape.518), calls=%async_computation | async-start | bytes 3145728 | tf_op jit(solution)/shard_map/all_to_all | solution.py:157
  34.5 1.3 fusion.68
  35.8 1.3 fusion.77
  40.9 13.8 %all-to-all-done = bf16[8,2,49152]{2,1,0:T(2,128)(2,1)S(1)} async-done(((bf16[8,2,49152]{2,1,0:T(2,128)(2,1)}), bf16[8,2,49152]{2,1,0:T(2,128)(2,1)S(1)}, u32[]{:S(2)}, u32[]{:S(2)}) %all-to-all-start) | async-done | bytes 1572896 | tf_op jit(solution)/shard_map/all_to_all | solution.py:157
  54.7 5.4 %reshape.519 = bf16[768,1,8,2,2,32]{5,4,3,2,1,0:T(2,128)(2,1)} reshape(bf16[8,2,49152]{2,1,0:T(2,128)(2,1)S(1)} %all-to-all-done) | data formatting | bytes 3145728
  60.2 11.0 %copy.35 = bf16[32,8,2,1,2,8,96]{6,5,4,1,2,0,3:T(8,128)(2,1)S(1)} copy(bf16[32,8,2,1,2,8,96]{0,4,2,1,6,5,3:T(2,128)(2,1)} %bitcast.164) | data formatting | bytes 3145728 | tf_op jit(solution)/shard_map/all_to_all | solution.py:157
  71.1 86.1 %while.10 = (s32[]{:T(128)}, bf16[32,4,2,8,2,96]{5,4,2,1,0,3:T(2,128)(2,1)}, bf16[32,8,2,8,2,96]{5,3,4,1,2,0:T(8,128)(2,1)S(1)}, bf16[2,8,2,1536]{3,1,2,0:T(8,12...) while((s32[]{:T(128)}, bf16[32,4,2,8,2,96]{5,4,2,1,0,3:T(2,128)(2,1)}, ...), condition=%wide.region_1.2_spmd, body=%wide.region_0.1_spmd.sunk | while | flops 122105856 | bytes 15680073 | solution.py:158
  71.2 0.8 convolution_bitcast_fusion.6
  73.8 0.8 convolution_bitcast_fusion.6
  76.5 0.8 convolution_bitcast_fusion.6
  79.2 0.8 convolution_bitcast_fusion.6
  92.7 0.8 convolution_bitcast_fusion.6
  98.1 0.8 convolution_bitcast_fusion.6
  100.8 0.8 convolution_bitcast_fusion.6
  103.5 0.8 convolution_bitcast_fusion.6
  108.9 0.8 convolution_bitcast_fusion.6
  114.3 0.8 convolution_bitcast_fusion.6
  119.6 0.8 convolution_bitcast_fusion.6
  130.4 0.8 convolution_bitcast_fusion.6
  133.1 0.8 convolution_bitcast_fusion.6
  135.8 0.8 convolution_bitcast_fusion.6
  141.1 0.8 convolution_bitcast_fusion.6
  143.8 0.8 convolution_bitcast_fusion.6
  146.5 0.8 convolution_bitcast_fusion.6
  149.2 0.8 convolution_bitcast_fusion.6
  151.9 0.8 convolution_bitcast_fusion.6
  157.3 3.7 %all-to-all-start.1 = ((bf16[32,4,2,8,2,96]{5,4,2,1,0,3:T(2,128)(2,1)}), bf16[32,4,2,8,2,96]{5,4,2,1,0,3:T(2,128)(2,1)S(1)}, u32[]{:S(2)}, u32[]{:S(2)}) async-start(bf16[32,4,2,8,2,96]{5,4,2,1,0,3:T(2,128)(2,1)} %get-tuple-element.32), calls=%async_computation.1 | async-start | bytes 2097152 | tf_op jit(solution)/shard_map/all_to_all | solution.py:159
  161.4 14.9 %all-to-all-done.1 = bf16[32,4,2,8,2,96]{5,4,2,1,0,3:T(2,128)(2,1)S(1)} async-done(((bf16[32,4,2,8,2,96]{5,4,2,1,0,3:T(2,128)(2,1)}), bf16[32,4,2,8,2,96]{5,4,2,1,0,3:T(2,128)(2,1)S(1)}, u32[]{:S(2)}, u32[]{:S(2)}) %all-to-all-start.1) | async-done | bytes 786464 | tf_op jit(solution)/shard_map/all_to_all | solution.py:159
  177.0 0.9 reshape.509
  177.9 2.1 fusion.13
  180.0 1.0 fusion.22
  181.0 2.9 %copy.42 = f32[4,2,32,528]{2,1,0,3:T(2,128)S(1)} copy(f32[4,2,32,528]{3,2,1,0:T(8,128)} %fusion.22) | data formatting | bytes 1081344 | tf_op jit(solution)/shard_map/mul | solution.py:172
  183.9 2.9 %reshape.520 = f32[4,1,33792]{2,1,0:T(1,128)} reshape(f32[528,4,2,32]{3,2,1,0:T(2,128)S(1)} %bitcast.165) | data formatting | bytes 1081344
  186.8 4.9 %all-to-all-start.2 = ((f32[4,1,33792]{2,1,0:T(1,128)}), f32[4,1,33792]{2,1,0:T(1,128)S(1)}, u32[]{:S(2)}, u32[]{:S(2)}) async-start(f32[4,1,33792]{2,1,0:T(1,128)} %reshape.520), calls=%async_computation.2 | async-start | bytes 1081344 | tf_op jit(solution)/shard_map/all_to_all | solution.py:173
  191.7 1.4 fusion.85
  194.1 9.6 %all-to-all-done.2 = f32[4,1,33792]{2,1,0:T(1,128)S(1)} async-done(((f32[4,1,33792]{2,1,0:T(1,128)}), f32[4,1,33792]{2,1,0:T(1,128)S(1)}, u32[]{:S(2)}, u32[]{:S(2)}) %all-to-all-start.2) | async-done | bytes 540704 | tf_op jit(solution)/shard_map/all_to_all | solution.py:173
  204.2 2.2 reduce.1
  206.4 1.9 reshape.521
  208.4 3.0 %copy.43 = f32[4,2,32,4,132]{4,2,3,1,0:T(8,128)} copy(f32[4,2,32,4,132]{2,1,0,4,3:T(2,128)S(1)} %bitcast.166) | data formatting | bytes 1081344 | tf_op jit(solution)/shard_map/all_to_all | solution.py:173
  211.4 3.2 %fusion.15 = f32[4,2,128,132]{2,3,1,0:T(8,128)S(1)} fusion(f32[4,2,128,132]{3,2,1,0:T(8,128)} %bitcast.171, f32[4,128,132]{1,2,0:T(8,128)S(1)} %copy-done.6, s32[128]{0:T(128)S(1)} %iota_add_fusion.1), kind=kOutput, calls=%fused_computation.32 | convolution fusion | flops 207917056 | bytes 1352192 | tf_op jit(solution)/shard_map/jk,fcks->fcjs/dot_general | solution.py:106
  214.5 0.9 convolution_bitcast_fusion.3
  216.1 26.7 %all_to_all.69 = f32[4,2,128,132]{3,1,0,2:T(2,128)S(1)} all-to-all(f32[4,2,128,132]{3,1,0,2:T(2,128)S(1)} %copy.45), channel_id=1, replica_groups=mesh['row'=4,'ma'=8] {'row'}, dimensions={2} | all-to-all | bytes 1081344 | tf_op jit(solution)/shard_map/all_to_all | solution.py:185
  244.5 0.9 broadcast_multiply_fusion
  (209 shorter events, 81.8 us)
Async XLA Ops:
  0.0 4.5 %copy-start = (bf16[528,768]{1,0:T(8,128)(2,1)S(1)}, bf16[528,768]{1,0:T(8,128)(2,1)}, u32[]{:S(2)}) copy-start(bf16[528,768]{1,0:T(8,128)(2,1)} %param.10) | copy-start | bytes 2433028
  2.1 0.6 copy-start.10
  4.5 35.0 %copy-start.1 = (f32[4,2,32,528]{3,2,1,0:T(8,128)}, f32[4,2,32,528]{3,2,1,0:T(8,128)S(1)}, u32[]{:S(2)}) copy-start(f32[4,2,32,528]{3,2,1,0:T(8,128)S(1)} %get-tuple-element.47) | copy-start | bytes 1622020
  5.3 1.1 copy-start.16
  28.4 5.3 %copy-start.12 = (s32[8]{0:T(128)S(1)}, s32[8]{0:T(128)}, u32[]{:S(2)}) copy-start(s32[8]{0:T(128)} %param.12) | copy-start | bytes 100
  28.4 26.3 %all-to-all-start = ((bf16[8,2,49152]{2,1,0:T(2,128)(2,1)}), bf16[8,2,49152]{2,1,0:T(2,128)(2,1)S(1)}, u32[]{:S(2)}, u32[]{:S(2)}) async-start(bf16[8,2,49152]{2,1,0:T(2,128)(2,1)} %reshape.518), calls=%async_computation | async-start | bytes 3145728 | tf_op jit(solution)/shard_map/all_to_all | solution.py:157
  60.2 11.0 %copy-start.7 = (bf16[2,8,2,1536]{3,1,2,0:T(8,128)(2,1)S(1)}, bf16[2,8,2,1536]{3,1,2,0:T(8,128)(2,1)}, u32[]{:S(2)}) copy-start(bf16[2,8,2,1536]{3,1,2,0:T(8,128)(2,1)} %fusion.27) | copy-start | bytes 294916
  157.2 3.7 %copy-start.3 = (f32[1,2,32,1,528]{4,2,1,3,0:T(8,128)S(1)}, f32[1,2,32,1,528]{4,2,1,3,0:T(8,128)}, u32[]{:S(2)}) copy-start(f32[1,2,32,1,528]{4,2,1,3,0:T(8,128)} %get-tuple-element.54) | copy-start | bytes 405508
  157.2 3.9 %copy-start.4 = (f32[1,32,1,528]{3,1,0,2:T(8,128)S(1)}, f32[1,32,1,528]{3,1,0,2:T(8,128)}, u32[]{:S(2)}) copy-start(f32[1,32,1,528]{3,1,0,2:T(8,128)} %get-tuple-element.61) | copy-start | bytes 202756
  157.3 3.9 %copy-start.5 = (f32[1,32,1,528]{3,1,2,0:T(8,128)S(1)}, f32[1,32,1,528]{3,1,2,0:T(8,128)}, u32[]{:S(2)}) copy-start(f32[1,32,1,528]{3,1,2,0:T(8,128)} %get-tuple-element.76) | copy-start | bytes 202756
  157.3 3.9 %copy-start.8 = (f32[528]{0:T(1024)S(1)}, f32[528]{0:T(1024)}, u32[]{:S(2)}) copy-start(f32[528]{0:T(1024)} %get-tuple-element.75) | copy-start | bytes 6340
  157.3 3.9 %copy-start.9 = (f32[528]{0:T(1024)S(1)}, f32[528]{0:T(1024)}, u32[]{:S(2)}) copy-start(f32[528]{0:T(1024)} %fusion.77) | copy-start | bytes 6340
  157.3 19.0 %all-to-all-start.1 = ((bf16[32,4,2,8,2,96]{5,4,2,1,0,3:T(2,128)(2,1)}), bf16[32,4,2,8,2,96]{5,4,2,1,0,3:T(2,128)(2,1)S(1)}, u32[]{:S(2)}, u32[]{:S(2)}) async-start(bf16[32,4,2,8,2,96]{5,4,2,1,0,3:T(2,128)(2,1)} %get-tuple-element.32), calls=%async_computation.1 | async-start | bytes 2097152 | tf_op jit(solution)/shard_map/all_to_all | solution.py:159
  176.3 1.6 copy-start.11
  177.9 2.1 copy-start.2
  177.9 2.1 copy-start.15
  183.9 9.3 %copy-start.14 = (f32[128]{0:T(128)S(1)}, f32[128]{0:T(128)}, u32[]{:S(2)}) copy-start(f32[128]{0:T(128)} %multiply_multiply_fusion.2) | copy-start | bytes 1540
  183.9 9.4 %copy-start.13 = (f32[4]{0:T(128)S(1)}, f32[4]{0:T(128)}, u32[]{:S(2)}) copy-start(f32[4]{0:T(128)} %param.13) | copy-start | bytes 52
  186.8 16.9 %all-to-all-start.2 = ((f32[4,1,33792]{2,1,0:T(1,128)}), f32[4,1,33792]{2,1,0:T(1,128)S(1)}, u32[]{:S(2)}, u32[]{:S(2)}) async-start(f32[4,1,33792]{2,1,0:T(1,128)} %reshape.520), calls=%async_computation.2 | async-start | bytes 1081344 | tf_op jit(solution)/shard_map/all_to_all | solution.py:173
  208.3 3.0 %copy-start.6 = (f32[4,128,132]{1,2,0:T(8,128)S(1)}, f32[4,128,132]{1,2,0:T(8,128)}, u32[]{:S(2)}) copy-start(f32[4,128,132]{1,2,0:T(8,128)} %multiply_add_fusion) | copy-start | bytes 811012
where the time goes:
time: 248 us; the launch traced here: 245 us
  local copies, waits for them, and re-layouts  77.7 us (31%)
  matrix products  49.3 us (20%)
  waiting for transfers between devices  38.4 us (15%)
  other arithmetic  36.6 us (15%)
  blocking collectives  26.7 us (11%)
  starting transfers between devices  13.9 us (6%)
    all_to_all x1, blocking collectives, local(): lax.all_to_all(solved, 'row', split_axis=2, concat_axis=3, tiled=True)  26.7 us
    dot_general x32, matrix products, one_radius(): jnp.einsum('qcpjt,cpjk->qtk', radius_block, synthesis, preferred_element_...  25.6 us
    another operation x65, other arithmetic  22.9 us
    unnamed x38, local copies, waits for them, and re-layouts  21.4 us
    dynamic_update_slice x32, local copies, waits for them, and re-layouts, local(): computed = lax.map(one_radius, latitudes)  20.8 us
    dot_general x32, matrix products, one_radius(): jnp.einsum('ftk,cpjk->fcpjt', products, analysis_fourier, preferred_eleme...  16 us
    all_to_all x1, waiting for transfers between devices, local(): lax.all_to_all(computed, 'ma', split_axis=3, concat_axis=5, tiled=True)  14.9 us
    all_to_all x1, waiting for transfers between devices, local(): lax.all_to_all(grid_spectra, 'ma', split_axis=5, concat_axis=3, tiled=True)  13.8 us
  transfers between devices with their start and end apart: 3, of which 3 were waited for; matrix products, arithmetic and copies ran while one was open for 4% of the time, Pallas kernels for 0%

commit v1 on v0

v1 whole, which is shorter than its diff:
```python
import functools

import jax
import jax.numpy as jnp
from jax import lax
from jax.experimental import pallas as pl
from jax.experimental.pallas import tpu as pltpu
from jax.sharding import PartitionSpec as P

LMAX = 511
ROTATION = 2.0
SHELL_RADIUS = 16.0
RADII = 8
FAR = 1 << 20
VMEM_LIMIT = 48 * 1024 * 1024


def slot_rows(lowest, slots):
    slot = lax.broadcasted_iota(jnp.int32, (1, slots), 1)
    first = slot < LMAX + 1 - lowest
    held = slot < LMAX + 2
    second = jnp.logical_and(jnp.logical_not(first), held)
    degree = jnp.where(first, lowest + slot, slot - 1)
    order = jnp.where(first, lowest, LMAX - lowest)
    return first, second, held, degree, order


def greet(axis_sizes):
    barrier = pltpu.get_barrier_semaphore()
    total = 0
    for axis, size in axis_sizes:
        me = lax.axis_index(axis)
        for k in range(1, size):
            pl.semaphore_signal(
                barrier, inc=1, device_id={axis: lax.rem(me + k, size)},
                device_id_type=pl.DeviceIdType.MESH,
            )
        total += size - 1
    pl.semaphore_wait(barrier, total)


def forward_kernel(n, pair, spectra, dtheta, dphi, out, send, send_sem, recv_sem):
    greet([("ma", n)])
    me = lax.axis_index("ma")
    slots = spectra.shape[3]
    radii = RADII
    halves = n * radii // spectra.shape[2]
    width = dtheta.shape[1] // halves
    lowest = pair[me]
    first, second, _, _, _ = slot_rows(lowest, slots)
    keep = jnp.where(lowest == 0, 0.0, 1.0).astype(jnp.float32)

    def block_for(e):
        group = e // halves
        half = lax.rem(e, halves)
        x = spectra[:, :, pl.ds(pl.multiple_of(group * radii, radii), radii), :]
        x = x.reshape(8 * radii, slots)
        lhs = jnp.concatenate([jnp.where(first, x, 0.0), jnp.where(second, x, 0.0)], axis=0)
        lhs = lhs.astype(jnp.bfloat16)
        columns = pl.ds(pl.multiple_of(half * width, 128), width)
        t = jnp.dot(lhs, dtheta[:, columns], preferred_element_type=jnp.float32)
        d = jnp.dot(lhs, dphi[:, columns], preferred_element_type=jnp.float32)
        t = t.reshape(2, 4, 2, radii, width)
        d = d.reshape(2, 4, 2, radii, width)
        parts = []
        for j in range(2):
            z_t, w_t, s_t, a_t = (t[j, f] for f in range(4))
            z_d, w_d, s_d, a_d = (d[j, f] for f in range(4))
            pieces = [
                (w_t[0] + z_d[1], w_t[1] - z_d[0]),
                (z_t[0] - w_d[1], z_t[1] + w_d[0]),
                (s_t[0], s_t[1]),
                (-s_d[1], s_d[0]),
                (a_d[1], -a_d[0]),
                (a_t[0], a_t[1]),
            ]
            for real, imag in pieces:
                parts += [real, imag * keep if j == 0 else imag]
        return jnp.concatenate(parts, axis=0).astype(jnp.bfloat16)

    def copy_to(e, source):
        return pltpu.make_async_remote_copy(
            src_ref=send.at[e], dst_ref=out.at[source],
            send_sem=send_sem.at[e], recv_sem=recv_sem.at[source],
            device_id={"ma": e}, device_id_type=pl.DeviceIdType.MESH,
        )

    def push(k, carry):
        e = lax.rem(me + k, n)
        send[e] = block_for(e)
        copy_to(e, me).start()
        return carry

    lax.fori_loop(1, n, push, 0)
    out[me] = block_for(me)

    def finish(k, carry):
        e = lax.rem(me + k, n)
        source = lax.rem(me + n - k, n)
        copy_to(e, source).wait_send()
        copy_to(e, source).wait_recv()
        return carry

    lax.fori_loop(1, n, finish, 0)


def triad_kernel(n, partner, x, out, states, list_a, list_b):
    orders = 2 * n
    signed = 2 * orders
    radii, width = states.shape[2], states.shape[3]

    def unpack(g, carry):
        block = x[g].astype(jnp.float32).reshape(2, 6, 2, radii, width)
        for j in range(2):
            for q in range(6):
                real, imag = block[j, q, 0], block[j, q, 1]
                states[2 * g + j, 2 * q] = real
                states[2 * g + j, 2 * q + 1] = imag
                states[orders + 2 * g + j, 2 * q] = real
                states[orders + 2 * g + j, 2 * q + 1] = -imag
        return carry

    lax.fori_loop(0, n, unpack, 0)

    def one_order(t, carry):
        def gather(s, count):
            b = partner[t * signed + s]
            list_a[count] = s
            list_b[count] = b
            return count + jnp.where(b >= 0, 1, 0)

        count = lax.fori_loop(0, signed, gather, 0, unroll=8)

        def add(i, total):
            a, b = list_a[i], list_b[i]

            def mul(p, q):
                pr, pi = states[a, 2 * p], states[a, 2 * p + 1]
                qr, qi = states[b, 2 * q], states[b, 2 * q + 1]
                return pr * qr - pi * qi, pr * qi + pi * qr

            ut, up, st, sp, bt, bp = range(6)
            plan = (
                ((bt, bp, 1), (ut, up, -1)),
                ((bp, bp, 1), (bt, bt, -1), (up, up, -1), (ut, ut, 1)),
                ((ut, st, 1), (up, sp, 1)),
                ((ut, bp, 1), (up, bt, -1)),
            )
            new = list(total)
            for f, terms in enumerate(plan):
                for p, q, sign in terms:
                    real, imag = mul(p, q)
                    if sign > 0:
                        new[2 * f] += real
                        new[2 * f + 1] += imag
                    else:
                        new[2 * f] -= real
                        new[2 * f + 1] -= imag
            return tuple(new)

        zero = jnp.zeros((radii, width), jnp.float32)
        total = lax.fori_loop(0, count, add, (zero,) * 8)
        scale = (1.0, 1.0, 0.5, 0.5, -1.0, -1.0, -1.0, -1.0)
        rows = jnp.concatenate([v * c for v, c in zip(total, scale)], axis=0)
        out[t] = rows.astype(jnp.bfloat16)
        return carry

    lax.fori_loop(0, orders, one_order, 0)


def backward_kernel(
    n, rows_count, pair, diffusivity, y, spectra, analysis, out,
    got, edges, right, send_sem, recv_sem, edge_send, edge_recv,
):
    greet([("ma", n), ("row", rows_count)])
    me = lax.axis_index("ma")
    row = lax.axis_index("row")
    slots = spectra.shape[3]
    points = spectra.shape[2]
    radii = RADII
    groups = points // radii
    halves = n // groups
    width = analysis.shape[1] // halves

    def copy_to(e, source):
        return pltpu.make_async_remote_copy(
            src_ref=y.at[e], dst_ref=got.at[source],
            send_sem=send_sem.at[e], recv_sem=recv_sem.at[source],
            device_id={"ma": e}, device_id_type=pl.DeviceIdType.MESH,
        )

    def push(k, carry):
        e = lax.rem(me + k, n)
        copy_to(e, me).start()
        return carry

    lax.fori_loop(1, n, push, 0)
    got[me] = y[me]

    lowest = pair[me]
    first, second, held, degree, order = slot_rows(lowest, slots)
    alive = held.astype(jnp.float32)
    l = degree.astype(jnp.float32)
    m = order.astype(jnp.float32)
    lower = jnp.sqrt((l * l - m * m) * alive / jnp.maximum(4.0 * l * l - 1.0, 1.0)) * ROTATION
    u = l + 1.0
    upper = jnp.sqrt(jnp.maximum((u * u - m * m) / (4.0 * u * u - 1.0), 0.0))
    upper = jnp.where(degree < LMAX, upper * alive, 0.0) * ROTATION
    spin = ROTATION * m / (l * (l + 1.0) + 2.0) * alive

    def couple(v):
        edge = jnp.zeros((points, 1), jnp.float32)
        below = jnp.concatenate([edge, v[:, : slots - 1]], axis=1)
        above = jnp.concatenate([v[:, 1:], edge], axis=1)
        return lower * below + upper * above

    z0, z1 = (jnp.where(held, spectra[0, c], 0.0) for c in range(2))
    w0, w1 = (jnp.where(held, spectra[1, c], 0.0) for c in range(2))
    right[0, 0] = z0 - spin * z1 + couple(w0) * alive
    right[0, 1] = z1 + spin * z0 + couple(w1) * alive
    right[1, 0] = w0 - spin * w1 - couple(z0) * alive
    right[1, 1] = w1 + spin * w0 - couple(z1) * alive
    for f in (2, 3):
        for c in range(2):
            right[f, c] = jnp.where(held, spectra[f, c], 0.0)

    all_points = points * rows_count
    rho, log_rho, inner = [], [], []
    for f in range(4):
        off = diffusivity[f] * float((all_points + 1) ** 2)
        half_excess = (1.0 + diffusivity[f] * (l * (l + 1.0) / SHELL_RADIUS**2)) / (2.0 * off)
        root = jnp.sqrt(half_excess * half_excess + 2.0 * half_excess)
        inverse = 1.0 + half_excess + root
        rho.append(1.0 / inverse)
        log_rho.append(-jnp.log(inverse))
        inner.append(1.0 / (2.0 * off * root))
    at = lax.broadcasted_iota(jnp.int32, (points, slots), 0)

    def finish(source):
        @pl.when(source != me)
        def _():
            copy_to(source, source).wait_recv()

    contract = (((1,), (1,)), ((), ()))
    for g in range(groups):
        total = jnp.zeros((16 * radii, slots), jnp.float32)
        for h in range(halves):
            finish(halves * g + h)
            total += lax.dot_general(
                got[halves * g + h].reshape(16 * radii, width),
                analysis[:, h * width : (h + 1) * width],
                contract, preferred_element_type=jnp.float32,
            )
        total = total.reshape(2, 4, 2, radii, slots)
        added = jnp.where(first, total[0], jnp.where(second, total[1], 0.0))
        right[:, :, g * radii : (g + 1) * radii, :] += added

    last, start = [], []
    for f in range(4):
        for c in range(2):
            b = right[f, c]
            ahead, back = b, b
            power = rho[f]
            step = 1
            while step < points:
                ahead += power * jnp.where(at >= step, pltpu.roll(ahead, step, 0), 0.0)
                back += power * jnp.where(
                    at < points - step, pltpu.roll(back, points - step, 0), 0.0
                )
                power = power * power
                step *= 2
            right[f, c] = inner[f] * (ahead + back - b)
            last.append(ahead[points - 1 : points])
            start.append(back[0:1])
    edges[row] = jnp.concatenate(last + start, axis=0)

    def edge_copy(e, source):
        return pltpu.make_async_remote_copy(
            src_ref=edges.at[row], dst_ref=edges.at[source],
            send_sem=edge_send.at[e], recv_sem=edge_recv.at[source],
            device_id={"row": e}, device_id_type=pl.DeviceIdType.MESH,
        )

    for k in range(1, rows_count):
        edge_copy(lax.rem(row + k, rows_count), row).start()

    def drain(k, carry):
        copy_to(lax.rem(me + k, n), me).wait_send()
        return carry

    lax.fori_loop(1, n, drain, 0)
    for k in range(1, rows_count):
        edge_copy(lax.rem(row + k, rows_count), lax.rem(row + rows_count - k, rows_count)).wait()

    ahead_in = [0.0] * 4
    back_in = [0.0] * 4
    ahead_all = [0.0] * 4
    back_all = [0.0] * 4
    for e in range(rows_count):
        block = edges[e]
        for f in range(4):
            f_e = block[2 * f : 2 * f + 2]
            g_e = block[8 + 2 * f : 10 + 2 * f]
            gap = (row - 1 - e) * points
            weight = jnp.where(gap >= 0, jnp.exp(log_rho[f] * jnp.maximum(gap, 0).astype(jnp.float32)), 0.0)
            ahead_in[f] += weight * f_e
            gap = (e - row - 1) * points
            weight = jnp.where(gap >= 0, jnp.exp(log_rho[f] * jnp.maximum(gap, 0).astype(jnp.float32)), 0.0)
            back_in[f] += weight * g_e
            ahead_all[f] += jnp.exp(log_rho[f] * float((rows_count - 1 - e) * points)) * f_e
            back_all[f] += jnp.exp(log_rho[f] * float(e * points)) * g_e
    near = (at + 1).astype(jnp.float32)
    far = (points - at).astype(jnp.float32)
    for f in range(4):
        span = jnp.exp(log_rho[f] * float(all_points + 1))
        low = inner[f] * rho[f] * back_all[f]
        high = inner[f] * rho[f] * ahead_all[f]
        scale = 1.0 / (1.0 - span * span)
        alpha = (span * high - low) * scale
        beta = (span * low - high) * scale
        before = (row * points).astype(jnp.float32)
        after = ((rows_count - 1 - row) * points).astype(jnp.float32)
        left = inner[f] * ahead_in[f] + alpha * jnp.exp(log_rho[f] * before)
        rest = inner[f] * back_in[f] + beta * jnp.exp(log_rho[f] * after)
        rise = jnp.exp(log_rho[f] * near)
        fall = jnp.exp(log_rho[f] * far)
        for c in range(2):
            value = right[f, c] + left[c : c + 1] * rise + rest[c : c + 1] * fall
            out[f, c] = jnp.where(held, value, 0.0)


def triad_table(pair_index):
    orders = jnp.stack([pair_index, LMAX - pair_index], axis=1).reshape(-1)
    signed = jnp.concatenate([orders, jnp.where(orders == 0, FAR, -orders)])
    need = orders[:, None] - signed[None, :]
    match = need[:, :, None] == signed[None, None, :]
    at = jnp.arange(signed.shape[0], dtype=jnp.int32) + 1
    return (jnp.sum(jnp.where(match, at, 0), axis=2) - 1).reshape(-1)


def local(n, rows_count, spectra, dtheta, dphi, analysis, pair_index, diffusivity):
    points, slots = spectra.shape[2], spectra.shape[3]
    radii = RADII
    halves = n * radii // points
    width = -(-dtheta.shape[1] // (128 * halves)) * 128
    extra = width * halves - dtheta.shape[1]
    if extra:
        dtheta, dphi, analysis = (jnp.pad(v, ((0, 0), (0, extra))) for v in (dtheta, dphi, analysis))
    vmem = pl.BlockSpec(memory_space=pltpu.VMEM)
    smem = pl.BlockSpec(memory_space=pltpu.SMEM)
    partner = triad_table(pair_index)
    grid = pl.pallas_call(
        functools.partial(forward_kernel, n),
        out_shape=jax.ShapeDtypeStruct((n, 24 * radii, width), jnp.bfloat16),
        in_specs=[smem, vmem, vmem, vmem],
        out_specs=vmem,
        scratch_shapes=[
            pltpu.VMEM((n, 24 * radii, width), jnp.bfloat16),
            pltpu.SemaphoreType.DMA((n,)),
            pltpu.SemaphoreType.DMA((n,)),
        ],
        compiler_params=pltpu.CompilerParams(
            collective_id=0, has_side_effects=True, vmem_limit_bytes=VMEM_LIMIT
        ),
        name="forward",
    )(pair_index, spectra, dtheta, dphi)
    products = pl.pallas_call(
        functools.partial(triad_kernel, n),
        out_shape=jax.ShapeDtypeStruct((2 * n, 8 * radii, width), jnp.bfloat16),
        in_specs=[smem, vmem],
        out_specs=vmem,
        scratch_shapes=[
            pltpu.VMEM((4 * n, 12, radii, width), jnp.float32),
            pltpu.SMEM((4 * n + 8,), jnp.int32),
            pltpu.SMEM((4 * n + 8,), jnp.int32),
        ],
        compiler_params=pltpu.CompilerParams(vmem_limit_bytes=VMEM_LIMIT),
        name="triads",
    )(partner, grid)
    products = products.reshape(n, 16 * radii, width)
    return pl.pallas_call(
        functools.partial(backward_kernel, n, rows_count),
        out_shape=jax.ShapeDtypeStruct(spectra.shape, jnp.float32),
        in_specs=[smem, smem, vmem, vmem, vmem],
        out_specs=vmem,
        scratch_shapes=[
            pltpu.VMEM((n, 16 * radii, width), jnp.bfloat16),
            pltpu.VMEM((rows_count, 16, slots), jnp.float32),
            pltpu.VMEM(spectra.shape, jnp.float32),
            pltpu.SemaphoreType.DMA((n,)),
            pltpu.SemaphoreType.DMA((n,)),
            pltpu.SemaphoreType.DMA((rows_count,)),
            pltpu.SemaphoreType.DMA((rows_count,)),
        ],
        compiler_params=pltpu.CompilerParams(
            collective_id=1, has_side_effects=True, vmem_limit_bytes=VMEM_LIMIT
        ),
        name="backward",
    )(pair_index, diffusivity, products, spectra, analysis)


def solution(mesh):
    n, rows_count = mesh.shape["ma"], mesh.shape["row"]
    return jax.shard_map(
        functools.partial(local, n, rows_count),
        mesh=mesh,
        in_specs=(
            P(None, None, "row", "ma"),
            P("ma", None),
            P("ma", None),
            P("ma", None),
            P(),
            P(),
        ),
        out_specs=P(None, None, "row", "ma"),
        check_vma=False,
    )
```

time: 248 us -> 53.7 us (0.22)
  local copies, waits for them, and re-layouts: 77.7 us -> 5.12 us
  matrix products: 49.3 us -> 0 us
  Pallas kernels: 0 us -> 45.8 us
  waiting for transfers between devices: 38.4 us -> 0 us
  other arithmetic: 36.6 us -> 1.94 us
  blocking collectives: 26.7 us -> 0 us
  starting transfers between devices: 13.9 us -> 0 us
    dot_general x69 -> x0, matrix products: 49.3 us -> none  [the longest x32 25.6 us: one_radius(): jnp.einsum('qcpjt,cpjk->qtk', radius_block, synthesis, preferred_element_...]
    pallas_call x0 -> x3, Pallas kernels: none -> 45.8 us  [the longest x1 20.4 us: local(): pl.pallas_call(functools.partial(backward_kernel, n, rows_count), out_sha...]
    all_to_all x3 -> x0, waiting for transfers between devices: 38.4 us -> none  [the longest x1 14.9 us: local(): lax.all_to_all(computed, 'ma', split_axis=3, concat_axis=5, tiled=True)]
    all_to_all x1 -> x0, blocking collectives: 26.7 us -> none  [local(): lax.all_to_all(solved, 'row', split_axis=2, concat_axis=3, tiled=True)]
    another operation x70 -> x2, other arithmetic: 23.6 us -> 1.32 us  [triad_table(): orders = jnp.stack([pair_index, LMAX - pair_index], axis=1).reshape(-1)]
    dynamic_update_slice x32 -> x0, local copies, waits for them, and re-layouts: 20.8 us -> none  [local(): computed = lax.map(one_radius, latitudes)]
    all_to_all x7 -> x0, local copies, waits for them, and re-layouts: 16.8 us -> none  [the longest x1 11 us: local(): lax.all_to_all(grid_spectra, 'ma', split_axis=5, concat_axis=3, tiled=True)]
    unnamed x38 -> x13, local copies, waits for them, and re-layouts: 21.4 us -> 4.88 us
  transfers between devices with their start and end apart: 3 -> 0, of which waited for: 3 -> 0; matrix products, arithmetic and copies ran while one was open for 4% -> 0% of each run, Pallas kernels for 0% -> 0%
where the time goes in v1:
time: 53.7 us; the launch traced here: 52.9 us
  Pallas kernels  45.8 us (85%)
  local copies, waits for them, and re-layouts  5.12 us (10%)
  other arithmetic  1.94 us (4%)
    pallas_call x1, Pallas kernels, local(): pl.pallas_call(functools.partial(backward_kernel, n, rows_count), out_sha...  20.4 us
    pallas_call x1, Pallas kernels, local(): pl.pallas_call(functools.partial(forward_kernel, n), out_shape=jax.ShapeD...  18.2 us
    pallas_call x1, Pallas kernels, local(): pl.pallas_call(functools.partial(triad_kernel, n), out_shape=jax.ShapeDty...  7.22 us
    unnamed x13, local copies, waits for them, and re-layouts  4.88 us
    another operation x2, other arithmetic, triad_table(): orders = jnp.stack([pair_index, LMAX - pair_index], axis=1).reshape(-1)  1.32 us

profile of v1, /device:TPU:0, one launch (start us, length us, event | category | flops | bytes accessed | tf_op | source)
XLA Modules:
  0.0 52.9 jit_solution(9479588378238017757)
XLA Ops:
  0.0 0.7 %subtract_bitcast_fusion = s32[8,1]{0,1:T(1,128)S(1)} fusion(s32[8]{0:T(128)} %pair.3), kind=kLoop, calls=%fused_computation.7 | loop fusion | flops 8 | bytes 64 | tf_op jit(solution)/shard_map/stack | solution.py:333
  0.7 0.7 %pad_add_fusion = s32[8,2]{0,1:T(2,128)S(1)} fusion(s32[8,1]{0,1:T(1,128)S(1)} %subtract_bitcast_fusion, s32[8,1]{0,1:T(1,128)} %bitcast.5), kind=kLoop, calls=%fused_computation.4 | loop fusion | flops 16 | bytes 128 | tf_op jit(solution)/shard_map/stack | solution.py:333
  1.3 0.1 copy.9
  1.4 0.1 sub.29
  1.5 0.1 pad_add_fusion.1
  1.6 0.1 broadcast_subtract_fusion
  1.6 0.5 select_reduce_fusion
  2.1 0.1 sub.34.partner
  2.2 0.0 copy-start
  2.2 1.1 %copy-done = f32[4,2,32,528]{3,2,1,0:T(8,128)S(1)} copy-done((f32[4,2,32,528]{3,2,1,0:T(8,128)S(1)}, f32[4,2,32,528]{3,2,1,0:T(8,128)}, u32[]{:S(2)}) %copy-start) | copy-done | bytes 540696
  3.3 0.0 copy-start.1
  3.3 1.1 %copy-done.1 = bf16[528,768]{1,0:T(8,128)(2,1)S(1)} copy-done((bf16[528,768]{1,0:T(8,128)(2,1)S(1)}, bf16[528,768]{1,0:T(8,128)(2,1)}, u32[]{:S(2)}) %copy-start.1) | copy-done | bytes 811032
  4.4 0.0 copy-start.2
  4.4 1.1 %copy-done.2 = bf16[528,768]{1,0:T(8,128)(2,1)S(1)} copy-done((bf16[528,768]{1,0:T(8,128)(2,1)S(1)}, bf16[528,768]{1,0:T(8,128)(2,1)}, u32[]{:S(2)}) %copy-start.2) | copy-done | bytes 811032
  5.6 0.0 copy-start.4
  5.6 0.7 %copy-done.4 = s32[8]{0:T(128)S(1)} copy-done((s32[8]{0:T(128)S(1)}, s32[8]{0:T(128)}, u32[]{:S(2)}) %copy-start.4) | copy-done | bytes 56
  6.2 18.2 %forward.1.x = bf16[8,192,384]{2,1,0:T(8,128)(2,1)S(1)} custom-call(s32[8]{0:T(128)S(1)} %copy-done.4, f32[4,2,32,528]{3,2,1,0:T(8,128)S(1)} %copy-done, bf16[528,768]{1,0:T(8,128)(2,1)S(1)} %copy-done.1, bf16[528,768]{1,0:T(8,128)(2,1)S(1)} %copy-done.2), custom_call_target="tpu_custom_call" | custom-call | tf_op jit(solution)/shard_map/forward/pallas_call | solution.py:352
  24.4 0.0 copy-start.3
  24.4 0.0 copy-start.5
  24.4 7.2 %triads.1 = bf16[16,64,384]{2,1,0:T(8,128)(2,1)S(1)} custom-call(s32[512]{0:T(512)S(1)} %sub.34.partner, bf16[8,192,384]{2,1,0:T(8,128)(2,1)S(1)} %forward.1.x), custom_call_target="tpu_custom_call" | custom-call | tf_op jit(solution)/shard_map/triads/pallas_call | solution.py:367
  31.7 0.0 copy-done.3
  31.7 0.0 copy-done.5
  31.7 20.4 %backward.1 = f32[4,2,32,528]{3,2,1,0:T(8,128)S(1)} custom-call(s32[8]{0:T(128)S(1)} %copy-done.4, f32[4]{0:T(128)S(1)} %copy-done.5, bf16[8,128,384]{2,1,0:T(8,128)(2,1)S(1)} %bitcast.4, f32[4,2,32,528]{3,2,1,0:T(8,128)S(1)} %copy-done, bf16[528,768]{1,0:T(8,128)(2,1)S(1)} %copy-done.3), custom_call_target="tpu_custom_call" | custom-call | tf_op jit(solution)/shard_map/backward/pallas_call | solution.py:381
  52.1 0.8 %copy.11 = f32[4,2,32,528]{3,2,1,0:T(8,128)} copy(f32[4,2,32,528]{3,2,1,0:T(8,128)S(1)} %backward.1) | data formatting | bytes 1081344
  (2 shorter events, 0.0 us)
Async XLA Ops:
  2.2 1.1 %copy-start = (f32[4,2,32,528]{3,2,1,0:T(8,128)S(1)}, f32[4,2,32,528]{3,2,1,0:T(8,128)}, u32[]{:S(2)}) copy-start(f32[4,2,32,528]{3,2,1,0:T(8,128)} %spectra.3) | copy-start | bytes 1622020
  3.3 1.1 %copy-start.1 = (bf16[528,768]{1,0:T(8,128)(2,1)S(1)}, bf16[528,768]{1,0:T(8,128)(2,1)}, u32[]{:S(2)}) copy-start(bf16[528,768]{1,0:T(8,128)(2,1)} %dtheta.1) | copy-start | bytes 2433028
  4.4 1.1 %copy-start.2 = (bf16[528,768]{1,0:T(8,128)(2,1)S(1)}, bf16[528,768]{1,0:T(8,128)(2,1)}, u32[]{:S(2)}) copy-start(bf16[528,768]{1,0:T(8,128)(2,1)} %dphi.1) | copy-start | bytes 2433028
  5.6 0.7 %copy-start.4 = (s32[8]{0:T(128)S(1)}, s32[8]{0:T(128)}, u32[]{:S(2)}) copy-start(s32[8]{0:T(128)} %pair.3) | copy-start | bytes 100
  24.4 7.3 %copy-start.3 = (bf16[528,768]{1,0:T(8,128)(2,1)S(1)}, bf16[528,768]{1,0:T(8,128)(2,1)}, u32[]{:S(2)}) copy-start(bf16[528,768]{1,0:T(8,128)(2,1)} %analysis.1) | copy-start | bytes 2433028
  24.4 7.3 %copy-start.5 = (f32[4]{0:T(128)S(1)}, f32[4]{0:T(128)}, u32[]{:S(2)}) copy-start(f32[4]{0:T(128)} %diffusivity.1) | copy-start | bytes 52

commit v2 on v1

--- a/solution.py
+++ b/solution.py
@@ -39,7 +39,32 @@
     pl.semaphore_wait(barrier, total)
 
 
-def forward_kernel(n, pair, spectra, dtheta, dphi, out, send, send_sem, recv_sem):
+def ring(me, n):
+    tall = n // 4
+
+    def target(dy, dx, dc):
+        y, x, c = me // 4, lax.rem(me // 2, 2), lax.rem(me, 2)
+        return lax.rem(y + dy, tall) * 4 + lax.rem(x + dx, 2) * 2 + lax.rem(c + dc, 2)
+
+    return target
+
+
+def far_first(n):
+    steps = [(dy, dx, dc) for dy in range(n // 4) for dx in range(2) for dc in range(2)]
+    return sorted(steps[1:], key=lambda d: (-((d[0] > 0) + d[1]), d[2], d[1]))
+
+
+def forward_kernel(
+    n, pair, spectra_hbm, dtheta_hbm, dphi_hbm, out, triads,
+    spectra, dtheta, dphi, send, load_sem, send_sem, recv_sem,
+):
+    loads = [
+        pltpu.make_async_copy(spectra_hbm, spectra, load_sem.at[0]),
+        pltpu.make_async_copy(dtheta_hbm, dtheta, load_sem.at[1]),
+        pltpu.make_async_copy(dphi_hbm, dphi, load_sem.at[2]),
+    ]
+    for load in loads:
+        load.start()
     greet([("ma", n)])
     me = lax.axis_index("ma")
     slots = spectra.shape[3]
@@ -49,6 +74,8 @@
     lowest = pair[me]
     first, second, _, _, _ = slot_rows(lowest, slots)
     keep = jnp.where(lowest == 0, 0.0, 1.0).astype(jnp.float32)
+    for load in loads:
+        load.wait()
 
     def block_for(e):
         group = e // halves
@@ -85,28 +112,72 @@
             device_id={"ma": e}, device_id_type=pl.DeviceIdType.MESH,
         )
 
-    def push(k, carry):
-        e = lax.rem(me + k, n)
+    target = ring(me, n)
+    for step in far_first(n):
+        e = target(*step)
         send[e] = block_for(e)
         copy_to(e, me).start()
-        return carry
-
-    lax.fori_loop(1, n, push, 0)
     out[me] = block_for(me)
+    list_triads(n, pair, triads)
 
     def finish(k, carry):
         e = lax.rem(me + k, n)
-        source = lax.rem(me + n - k, n)
-        copy_to(e, source).wait_send()
-        copy_to(e, source).wait_recv()
+        copy_to(e, e).wait_send()
+        copy_to(e, e).wait_recv()
         return carry
 
     lax.fori_loop(1, n, finish, 0)
 
 
-def triad_kernel(n, partner, x, out, states, list_a, list_b):
+def list_triads(n, pair, triads):
+    orders, signed = 2 * n, 4 * n
+
+    def signed_orders(shape, dim, parts):
+        index = lax.broadcasted_iota(jnp.int32, shape, dim)
+        place = lax.rem(index, orders)
+        value = jnp.zeros(shape, jnp.int32)
+        for g in range(n):
+            value = jnp.where(place == 2 * g, pair[g], value)
+            value = jnp.where(place == 2 * g + 1, LMAX - pair[g], value)
+        if parts == 1:
+            return value
+        value = jnp.where(index >= orders, jnp.where(value == 0, FAR, -value), value)
+        return jnp.where(index < signed, value, 3 * FAR)
+
+    as_b = signed_orders((signed, 1), 0, 2)
+    as_a = signed_orders((1, 128), 1, 2)
+    as_m = signed_orders((orders, 1), 0, 1)
+    need = as_m - as_a
+    found = jnp.zeros((orders, 128), jnp.float32)
+    for s in range(signed):
+        found = jnp.where(need == as_b[s : s + 1, :], float(s + 1), found)
+    valid = found > 0.0
+    earlier = lax.broadcasted_iota(jnp.int32, (128, 128), 0) < lax.broadcasted_iota(
+        jnp.int32, (128, 128), 1
+    )
+    ones = jnp.where(valid, 1.0, 0.0)
+    rank = jnp.dot(
+        ones.astype(jnp.bfloat16), jnp.where(earlier, 1.0, 0.0).astype(jnp.bfloat16),
+        preferred_element_type=jnp.float32,
+    )
+    lane = lax.broadcasted_iota(jnp.int32, (orders, 128), 1)
+    code = lane.astype(jnp.float32) * float(signed) + found - 1.0
+    rank = jnp.where(valid, rank, -1.0)
+
+    def place(s, table):
+        hit = jnp.sum(jnp.where(rank == s.astype(jnp.float32), code, 0.0), axis=1, keepdims=True)
+        return jnp.where(lane == s, hit, table)
+
+    table = lax.fori_loop(0, signed, place, jnp.zeros((orders, 128), jnp.float32))
+    triads[:, :128] = table.astype(jnp.int32)
+    count = jnp.sum(ones, axis=1, keepdims=True)
+    triads[:, 128:] = jnp.broadcast_to(count, (orders, 128)).astype(jnp.int32)
+
+
+def triad_kernel(n, triads, x, out, states):
     orders = 2 * n
     signed = 2 * orders
+    shift = signed.bit_length() - 1
     radii, width = states.shape[2], states.shape[3]
 
     def unpack(g, carry):
@@ -123,16 +194,12 @@
     lax.fori_loop(0, n, unpack, 0)
 
     def one_order(t, carry):
-        def gather(s, count):
-            b = partner[t * signed + s]
-            list_a[count] = s
-            list_b[count] = b
-            return count + jnp.where(b >= 0, 1, 0)
-
-        count = lax.fori_loop(0, signed, gather, 0, unroll=8)
+        count = triads[t, 128]
 
         def add(i, total):
-            a, b = list_a[i], list_b[i]
+            code = triads[t, i]
+            a = lax.shift_right_logical(code, shift)
+            b = code - a * signed
 
             def mul(p, q):
                 pr, pi = states[a, 2 * p], states[a, 2 * p + 1]
@@ -169,9 +236,16 @@
 
 
 def backward_kernel(
-    n, rows_count, pair, diffusivity, y, spectra, analysis, out,
-    got, edges, right, send_sem, recv_sem, edge_send, edge_recv,
+    n, rows_count, pair, diffusivity, y, spectra_hbm, analysis_hbm, out,
+    spectra, analysis, got, edges, right, carries,
+    load_sem, send_sem, recv_sem, edge_send, edge_recv,
 ):
+    loads = [
+        pltpu.make_async_copy(spectra_hbm, spectra, load_sem.at[0]),
+        pltpu.make_async_copy(analysis_hbm, analysis, load_sem.at[1]),
+    ]
+    for load in loads:
+        load.start()
     greet([("ma", n), ("row", rows_count)])
     me = lax.axis_index("ma")
     row = lax.axis_index("row")
@@ -189,12 +263,9 @@
             device_id={"ma": e}, device_id_type=pl.DeviceIdType.MESH,
         )
 
-    def push(k, carry):
-        e = lax.rem(me + k, n)
-        copy_to(e, me).start()
-        return carry
-
-    lax.fori_loop(1, n, push, 0)
+    target = ring(me, n)
+    for step in reversed(far_first(n)):
+        copy_to(target(*step), me).start()
     got[me] = y[me]
 
     lowest = pair[me]
@@ -208,6 +279,28 @@
     upper = jnp.where(degree < LMAX, upper * alive, 0.0) * ROTATION
     spin = ROTATION * m / (l * (l + 1.0) + 2.0) * alive
 
+    all_points = points * rows_count
+    field = lax.broadcasted_iota(jnp.int32, (8, 1), 0) // 2
+    nu = jnp.zeros((8, 1), jnp.float32)
+    for f in range(4):
+        nu = jnp.where(field == f, diffusivity[f], nu)
+    off = nu * float((all_points + 1) ** 2)
+    half_excess = (1.0 + nu * (l * (l + 1.0) / SHELL_RADIUS**2)) / (2.0 * off)
+    root = jnp.sqrt(half_excess * half_excess + 2.0 * half_excess)
+    inverse = 1.0 + half_excess + root
+    rho = 1.0 / inverse
+    log_rho = -jnp.log(inverse)
+    inner = 1.0 / (2.0 * off * root)
+    at = lax.broadcasted_iota(jnp.int32, (radii, slots), 0)
+    near = (at + 1).astype(jnp.float32)
+    far = (radii - at).astype(jnp.float32)
+
+    def power(exponent):
+        return jnp.exp(log_rho * exponent)
+
+    for load in loads:
+        load.wait()
+
     def couple(v):
         edge = jnp.zeros((points, 1), jnp.float32)
         below = jnp.concatenate([edge, v[:, : slots - 1]], axis=1)
@@ -224,55 +317,60 @@
         for c in range(2):
             right[f, c] = jnp.where(held, spectra[f, c], 0.0)
 
-    all_points = points * rows_count
-    rho, log_rho, inner = [], [], []
-    for f in range(4):
-        off = diffusivity[f] * float((all_points + 1) ** 2)
-        half_excess = (1.0 + diffusivity[f] * (l * (l + 1.0) / SHELL_RADIUS**2)) / (2.0 * off)
-        root = jnp.sqrt(half_excess * half_excess + 2.0 * half_excess)
-        inverse = 1.0 + half_excess + root
-        rho.append(1.0 / inverse)
-        log_rho.append(-jnp.log(inverse))
-        inner.append(1.0 / (2.0 * off * root))
-    at = lax.broadcasted_iota(jnp.int32, (points, slots), 0)
-
-    def finish(source):
-        @pl.when(source != me)
-        def _():
-            copy_to(source, source).wait_recv()
-
     contract = (((1,), (1,)), ((), ()))
-    for g in range(groups):
+    own_group = me // halves
+    for k in group_order(n, groups):
+        g = lax.rem(own_group // k[2] + k[0], groups // k[2]) * k[2] + lax.rem(
+            lax.rem(own_group, k[2]) + k[1], k[2]
+        )
         total = jnp.zeros((16 * radii, slots), jnp.float32)
         for h in range(halves):
-            finish(halves * g + h)
+            source = halves * g + h
+
+            @pl.when(source != me)
+            def _(source=source):
+                copy_to(source, source).wait_recv()
+
             total += lax.dot_general(
-                got[halves * g + h].reshape(16 * radii, width),
-                analysis[:, h * width : (h + 1) * width],
+                got[source], analysis[:, h * width : (h + 1) * width],
                 contract, preferred_element_type=jnp.float32,
             )
         total = total.reshape(2, 4, 2, radii, slots)
         added = jnp.where(first, total[0], jnp.where(second, total[1], 0.0))
-        right[:, :, g * radii : (g + 1) * radii, :] += added
-
-    last, start = [], []
-    for f in range(4):
-        for c in range(2):
-            b = right[f, c]
-            ahead, back = b, b
-            power = rho[f]
-            step = 1
-            while step < points:
-                ahead += power * jnp.where(at >= step, pltpu.roll(ahead, step, 0), 0.0)
-                back += power * jnp.where(
-                    at < points - step, pltpu.roll(back, points - step, 0), 0.0
-                )
-                power = power * power
-                step *= 2
-            right[f, c] = inner[f] * (ahead + back - b)
-            last.append(ahead[points - 1 : points])
-            start.append(back[0:1])
-    edges[row] = jnp.concatenate(last + start, axis=0)
+        rows = pl.ds(pl.multiple_of(g * radii, radii), radii)
+        last, start = [], []
+        for f in range(4):
+            scale = inner[2 * f : 2 * f + 1]
+            for c in range(2):
+                b = right[f, c, rows, :] + added[f, c]
+                ahead, back = b, b
+                ratio = rho[2 * f : 2 * f + 1]
+                step = 1
+                while step < radii:
+                    ahead += ratio * jnp.where(at >= step, pltpu.roll(ahead, step, 0), 0.0)
+                    back += ratio * jnp.where(
+                        at < radii - step, pltpu.roll(back, radii - step, 0), 0.0
+                    )
+                    ratio = ratio * ratio
+                    step *= 2
+                right[f, c, rows, :] = scale * (ahead + back - b)
+                last.append(ahead[radii - 1 : radii])
+                start.append(back[0:1])
+        carries[g, 0] = jnp.concatenate(last, axis=0)
+        carries[g, 1] = jnp.concatenate(start, axis=0)
+
+    hop = power(float(radii))
+    ahead_at, back_at = [], []
+    total = jnp.zeros((8, slots), jnp.float32)
+    for g in range(groups):
+        ahead_at.append(total)
+        total = hop * total + carries[g, 0]
+    edges[row, 0:8] = total
+    total = jnp.zeros((8, slots), jnp.float32)
+    for g in reversed(range(groups)):
+        back_at.insert(0, total)
+        total = hop * total + carries[g, 1]
+    edges[row, 8:16] = total
 
     def edge_copy(e, source):
         return pltpu.make_async_remote_copy(
@@ -284,58 +382,56 @@
     for k in range(1, rows_count):
         edge_copy(lax.rem(row + k, rows_count), row).start()
 
+    before = (row * points).astype(jnp.float32)
+    after = ((rows_count - 1 - row) * points).astype(jnp.float32)
+    span = power(float(all_points + 1))
+    scale = 1.0 / (1.0 - span * span)
+    to_start, to_end = power(before), power(after)
+    rise = [jnp.exp(log_rho[2 * f : 2 * f + 1] * near) for f in range(4)]
+    fall = [jnp.exp(log_rho[2 * f : 2 * f + 1] * far) for f in range(4)]
+    shifts = [power(float(k * points)) for k in range(rows_count)]
+    inside = [power(float(k * radii)) for k in range(groups)]
+
     def drain(k, carry):
         copy_to(lax.rem(me + k, n), me).wait_send()
         return carry
 
     lax.fori_loop(1, n, drain, 0)
     for k in range(1, rows_count):
-        edge_copy(lax.rem(row + k, rows_count), lax.rem(row + rows_count - k, rows_count)).wait()
-
-    ahead_in = [0.0] * 4
-    back_in = [0.0] * 4
-    ahead_all = [0.0] * 4
-    back_all = [0.0] * 4
+        e = lax.rem(row + k, rows_count)
+        edge_copy(e, e).wait()
+
+    zero = jnp.zeros((8, slots), jnp.float32)
+    ahead_in, back_in, ahead_all, back_all = zero, zero, zero, zero
     for e in range(rows_count):
-        block = edges[e]
+        f_e, g_e = edges[e, 0:8], edges[e, 8:16]
+        weight, reverse = zero, zero
+        for k in range(rows_count - 1):
+            weight = jnp.where(row - 1 - e == k, shifts[k], weight)
+            reverse = jnp.where(e - row - 1 == k, shifts[k], reverse)
+        ahead_in += weight * f_e
+        back_in += reverse * g_e
+        ahead_all += shifts[rows_count - 1 - e] * f_e
+        back_all += shifts[e] * g_e
+    low = inner * rho * back_all
+    high = inner * rho * ahead_all
+    left = inner * ahead_in + (span * high - low) * scale * to_start
+    rest = inner * back_in + (span * low - high) * scale * to_end
+    for g in range(groups):
+        here = left * inside[g] + inner * ahead_at[g]
+        there = rest * inside[groups - 1 - g] + inner * back_at[g]
         for f in range(4):
-            f_e = block[2 * f : 2 * f + 2]
-            g_e = block[8 + 2 * f : 10 + 2 * f]
-            gap = (row - 1 - e) * points
-            weight = jnp.where(gap >= 0, jnp.exp(log_rho[f] * jnp.maximum(gap, 0).astype(jnp.float32)), 0.0)
-            ahead_in[f] += weight * f_e
-            gap = (e - row - 1) * points
-            weight = jnp.where(gap >= 0, jnp.exp(log_rho[f] * jnp.maximum(gap, 0).astype(jnp.float32)), 0.0)
-            back_in[f] += weight * g_e
-            ahead_all[f] += jnp.exp(log_rho[f] * float((rows_count - 1 - e) * points)) * f_e
-            back_all[f] += jnp.exp(log_rho[f] * float(e * points)) * g_e
-    near = (at + 1).astype(jnp.float32)
-    far = (points - at).astype(jnp.float32)
-    for f in range(4):
-        span = jnp.exp(log_rho[f] * float(all_points + 1))
-        low = inner[f] * rho[f] * back_all[f]
-        high = inner[f] * rho[f] * ahead_all[f]
-        scale = 1.0 / (1.0 - span * span)
-        alpha = (span * high - low) * scale
-        beta = (span * low - high) * scale
-        before = (row * points).astype(jnp.float32)
-        after = ((rows_count - 1 - row) * points).astype(jnp.float32)
-        left = inner[f] * ahead_in[f] + alpha * jnp.exp(log_rho[f] * before)
-        rest = inner[f] * back_in[f] + beta * jnp.exp(log_rho[f] * after)
-        rise = jnp.exp(log_rho[f] * near)
-        fall = jnp.exp(log_rho[f] * far)
-        for c in range(2):
-            value = right[f, c] + left[c : c + 1] * rise + rest[c : c + 1] * fall
-            out[f, c] = jnp.where(held, value, 0.0)
-
-
-def triad_table(pair_index):
-    orders = jnp.stack([pair_index, LMAX - pair_index], axis=1).reshape(-1)
-    signed = jnp.concatenate([orders, jnp.where(orders == 0, FAR, -orders)])
-    need = orders[:, None] - signed[None, :]
-    match = need[:, :, None] == signed[None, None, :]
-    at = jnp.arange(signed.shape[0], dtype=jnp.int32) + 1
-    return (jnp.sum(jnp.where(match, at, 0), axis=2) - 1).reshape(-1)
+            for c in range(2):
+                i = 2 * f + c
+                value = right[f, c, g * radii : (g + 1) * radii, :]
+                value = value + here[i : i + 1] * rise[f] + there[i : i + 1] * fall[f]
+                out[f, c, g * radii : (g + 1) * radii, :] = jnp.where(held, value, 0.0)
+
+
+def group_order(n, groups):
+    inner = 2 if groups % 2 == 0 and n == 2 * groups else 1
+    steps = [(dy, dx, inner) for dy in range(groups // inner) for dx in range(inner)]
+    return sorted(steps, key=lambda d: (d[0] > 0) + d[1])
 
 
 def local(n, rows_count, spectra, dtheta, dphi, analysis, pair_index, diffusivity):
@@ -348,14 +444,23 @@
         dtheta, dphi, analysis = (jnp.pad(v, ((0, 0), (0, extra))) for v in (dtheta, dphi, analysis))
     vmem = pl.BlockSpec(memory_space=pltpu.VMEM)
     smem = pl.BlockSpec(memory_space=pltpu.SMEM)
-    partner = triad_table(pair_index)
-    grid = pl.pallas_call(
+    hbm = pl.BlockSpec(memory_space=pltpu.HBM)
+    shape = spectra.shape
+    table_shape = dtheta.shape
+    grid, triads = pl.pallas_call(
         functools.partial(forward_kernel, n),
-        out_shape=jax.ShapeDtypeStruct((n, 24 * radii, width), jnp.bfloat16),
-        in_specs=[smem, vmem, vmem, vmem],
-        out_specs=vmem,
+        out_shape=[
+            jax.ShapeDtypeStruct((n, 24 * radii, width), jnp.bfloat16),
+            jax.ShapeDtypeStruct((2 * n, 256), jnp.int32),
+        ],
+        in_specs=[smem, hbm, hbm, hbm],
+        out_specs=[vmem, vmem],
         scratch_shapes=[
+            pltpu.VMEM(shape, jnp.float32),
+            pltpu.VMEM(table_shape, jnp.bfloat16),
+            pltpu.VMEM(table_shape, jnp.bfloat16),
             pltpu.VMEM((n, 24 * radii, width), jnp.bfloat16),
+            pltpu.SemaphoreType.DMA((3,)),
             pltpu.SemaphoreType.DMA((n,)),
             pltpu.SemaphoreType.DMA((n,)),
         ],
@@ -371,22 +476,24 @@
         out_specs=vmem,
         scratch_shapes=[
             pltpu.VMEM((4 * n, 12, radii, width), jnp.float32),
-            pltpu.SMEM((4 * n + 8,), jnp.int32),
-            pltpu.SMEM((4 * n + 8,), jnp.int32),
         ],
         compiler_params=pltpu.CompilerParams(vmem_limit_bytes=VMEM_LIMIT),
         name="triads",
-    )(partner, grid)
+    )(triads, grid)
     products = products.reshape(n, 16 * radii, width)
     return pl.pallas_call(
         functools.partial(backward_kernel, n, rows_count),
         out_shape=jax.ShapeDtypeStruct(spectra.shape, jnp.float32),
-        in_specs=[smem, smem, vmem, vmem, vmem],
+        in_specs=[smem, smem, vmem, hbm, hbm],
         out_specs=vmem,
         scratch_shapes=[
+            pltpu.VMEM(shape, jnp.float32),
+            pltpu.VMEM(table_shape, jnp.bfloat16),
             pltpu.VMEM((n, 16 * radii, width), jnp.bfloat16),
             pltpu.VMEM((rows_count, 16, slots), jnp.float32),
-            pltpu.VMEM(spectra.shape, jnp.float32),
+            pltpu.VMEM(shape, jnp.float32),
+            pltpu.VMEM((points // radii, 2, 8, slots), jnp.float32),
+            pltpu.SemaphoreType.DMA((2,)),
             pltpu.SemaphoreType.DMA((n,)),
             pltpu.SemaphoreType.DMA((n,)),
             pltpu.SemaphoreType.DMA((rows_count,)),

time: 53.7 us -> 51.2 us (0.953)
  other arithmetic: 1.94 us -> 0 us
    pallas_call x1, Pallas kernels: 18.2 us -> 19.5 us  [local(): pl.pallas_call(functools.partial(forward_kernel, n), out_shape=[jax.Shape...]
    another operation x2 -> x0, other arithmetic: 1.32 us -> none  [triad_table(): orders = jnp.stack([pair_index, LMAX - pair_index], axis=1).reshape(-1)]
    pallas_call x1, Pallas kernels: 7.22 us -> 6.06 us  [local(): pl.pallas_call(functools.partial(triad_kernel, n), out_shape=jax.ShapeDty...]
    unnamed x13 -> x15, local copies, waits for them, and re-layouts: 4.88 us -> 4.88 us
where the time goes in v2:
time: 51.2 us; the launch traced here: 50.8 us
  Pallas kernels  45.8 us (89%)
  local copies, waits for them, and re-layouts  4.88 us (10%)
    pallas_call x1, Pallas kernels, local(): pl.pallas_call(functools.partial(backward_kernel, n, rows_count), out_sha...  20.2 us
    pallas_call x1, Pallas kernels, local(): pl.pallas_call(functools.partial(forward_kernel, n), out_shape=[jax.Shape...  19.5 us
    pallas_call x1, Pallas kernels, local(): pl.pallas_call(functools.partial(triad_kernel, n), out_shape=jax.ShapeDty...  6.06 us
    unnamed x15, local copies, waits for them, and re-layouts  4.88 us

profile of v2, /device:TPU:0, one launch (start us, length us, event | category | flops | bytes accessed | tf_op | source)
XLA Modules:
  0.0 50.8 jit_solution(6493056134621336375)
XLA Ops:
  0.0 0.0 copy-start
  0.0 1.1 %copy-done = f32[4,2,32,528]{3,2,1,0:T(8,128)S(1)} copy-done((f32[4,2,32,528]{3,2,1,0:T(8,128)S(1)}, f32[4,2,32,528]{3,2,1,0:T(8,128)}, u32[]{:S(2)}) %copy-start) | copy-done | bytes 540696
  1.1 0.0 copy-start.2
  1.1 1.1 %copy-done.2 = bf16[528,768]{1,0:T(8,128)(2,1)S(1)} copy-done((bf16[528,768]{1,0:T(8,128)(2,1)S(1)}, bf16[528,768]{1,0:T(8,128)(2,1)}, u32[]{:S(2)}) %copy-start.2) | copy-done | bytes 811032
  2.2 0.0 copy-start.3
  2.2 1.1 %copy-done.3 = bf16[528,768]{1,0:T(8,128)(2,1)S(1)} copy-done((bf16[528,768]{1,0:T(8,128)(2,1)S(1)}, bf16[528,768]{1,0:T(8,128)(2,1)}, u32[]{:S(2)}) %copy-start.3) | copy-done | bytes 811032
  3.4 0.0 copy-start.5
  3.4 0.7 %copy-done.5 = s32[8]{0:T(128)S(1)} copy-done((s32[8]{0:T(128)S(1)}, s32[8]{0:T(128)}, u32[]{:S(2)}) %copy-start.5) | copy-done | bytes 56
  4.0 19.5 %forward.1 = (bf16[8,192,384]{2,1,0:T(8,128)(2,1)S(1)}, s32[16,256]{1,0:T(8,128)S(1)}) custom-call(s32[8]{0:T(128)S(1)} %copy-done.5, f32[4,2,32,528]{3,2,1,0:T(8,128)S(1)} %copy-done, bf16[528,768]{1,0:T(8,128)(2,1)S(1)} %copy-done.2, bf16[528,768]{1,0:T(8,128)(2,1)S(1)} %copy-done.3), custom_call_target="tpu_custom_call" | custom-call | tf_op jit(solution)/shard_map/forward/pallas_call | solution.py:450
  23.5 0.0 copy-start.1
  23.6 0.0 copy-start.4
  23.6 0.0 copy-start.6
  23.6 6.1 %triads.1 = bf16[16,64,384]{2,1,0:T(8,128)(2,1)S(1)} custom-call(s32[16,256]{1,0:T(8,128)S(1)} %get-tuple-element.7.triads, bf16[8,192,384]{2,1,0:T(8,128)(2,1)S(1)} %get-tuple-element.8.x), custom_call_target="tpu_custom_call" | custom-call | tf_op jit(solution)/shard_map/triads/pallas_call | solution.py:472
  29.7 0.0 copy-done.1
  29.7 0.0 copy-done.4
  29.7 0.0 copy-done.6
  29.7 20.2 %backward.1 = f32[4,2,32,528]{3,2,1,0:T(8,128)S(1)} custom-call(s32[8]{0:T(128)S(1)} %copy-done.5, f32[4]{0:T(128)S(1)} %copy-done.6, bf16[8,128,384]{2,1,0:T(8,128)(2,1)S(1)} %bitcast.1, f32[4,2,32,528]{3,2,1,0:T(8,128)S(1)} %copy-done.1, bf16[528,768]{1,0:T(8,128)(2,1)S(1)} %copy-done.4), custom_call_target="tpu_custom_call" | custom-call | tf_op jit(solution)/shard_map/backward/pallas_call | solution.py:484
  49.9 0.8 %copy.8 = f32[4,2,32,528]{3,2,1,0:T(8,128)} copy(f32[4,2,32,528]{3,2,1,0:T(8,128)S(1)} %backward.1) | data formatting | bytes 1081344
Async XLA Ops:
  0.0 1.1 %copy-start = (f32[4,2,32,528]{3,2,1,0:T(8,128)S(1)}, f32[4,2,32,528]{3,2,1,0:T(8,128)}, u32[]{:S(2)}) copy-start(f32[4,2,32,528]{3,2,1,0:T(8,128)} %spectra_hbm.3) | copy-start | bytes 1622020
  1.1 1.1 %copy-start.2 = (bf16[528,768]{1,0:T(8,128)(2,1)S(1)}, bf16[528,768]{1,0:T(8,128)(2,1)}, u32[]{:S(2)}) copy-start(bf16[528,768]{1,0:T(8,128)(2,1)} %dtheta_hbm.1) | copy-start | bytes 2433028
  2.2 1.1 %copy-start.3 = (bf16[528,768]{1,0:T(8,128)(2,1)S(1)}, bf16[528,768]{1,0:T(8,128)(2,1)}, u32[]{:S(2)}) copy-start(bf16[528,768]{1,0:T(8,128)(2,1)} %dphi_hbm.1) | copy-start | bytes 2433028
  3.4 0.7 %copy-start.5 = (s32[8]{0:T(128)S(1)}, s32[8]{0:T(128)}, u32[]{:S(2)}) copy-start(s32[8]{0:T(128)} %pair.3) | copy-start | bytes 100
  23.5 6.1 %copy-start.1 = (f32[4,2,32,528]{3,2,1,0:T(8,128)S(1)}, f32[4,2,32,528]{3,2,1,0:T(8,128)}, u32[]{:S(2)}) copy-start(f32[4,2,32,528]{3,2,1,0:T(8,128)} %spectra_hbm.3) | copy-start | bytes 1622020
  23.6 6.1 %copy-start.4 = (bf16[528,768]{1,0:T(8,128)(2,1)S(1)}, bf16[528,768]{1,0:T(8,128)(2,1)}, u32[]{:S(2)}) copy-start(bf16[528,768]{1,0:T(8,128)(2,1)} %analysis_hbm.1) | copy-start | bytes 2433028
  23.6 6.1 %copy-start.6 = (f32[4]{0:T(128)S(1)}, f32[4]{0:T(128)}, u32[]{:S(2)}) copy-start(f32[4]{0:T(128)} %diffusivity.1) | copy-start | bytes 52

commit v3 on v2

v3 whole, which is shorter than its diff:
```python
import functools

import jax
import jax.numpy as jnp
from jax import lax
from jax.experimental import pallas as pl
from jax.experimental.pallas import tpu as pltpu
from jax.sharding import PartitionSpec as P

LMAX = 511
ROTATION = 2.0
SHELL_RADIUS = 16.0
RADII = 8
VMEM_LIMIT = 62 * 1024 * 1024


def slot_rows(lowest, slots):
    slot = lax.broadcasted_iota(jnp.int32, (1, slots), 1)
    first = slot < LMAX + 1 - lowest
    held = slot < LMAX + 2
    second = jnp.logical_and(jnp.logical_not(first), held)
    degree = jnp.where(first, lowest + slot, slot - 1)
    order = jnp.where(first, lowest, LMAX - lowest)
    return first, second, held, degree, order


def greet(axis_sizes):
    barrier = pltpu.get_barrier_semaphore()
    total = 0
    for axis, size in axis_sizes:
        me = lax.axis_index(axis)
        for k in range(1, size):
            pl.semaphore_signal(
                barrier, inc=1, device_id={axis: lax.rem(me + k, size)},
                device_id_type=pl.DeviceIdType.MESH,
            )
        total += size - 1
    pl.semaphore_wait(barrier, total)


def ring(me, n):
    tall = n // 4

    def target(dy, dx, dc):
        y, x, c = me // 4, lax.rem(me // 2, 2), lax.rem(me, 2)
        return lax.rem(y + dy, tall) * 4 + lax.rem(x + dx, 2) * 2 + lax.rem(c + dc, 2)

    return target


def far_first(n):
    steps = [(dy, dx, dc) for dy in range(n // 4) for dx in range(2) for dc in range(2)]
    return sorted(steps[1:], key=lambda d: (-((d[0] > 0) + d[1]), d[2], d[1]))


def step_kernel(
    n, rows_count, partner, pair, diffusivity, spectra_hbm, dtheta_hbm, dphi_hbm, analysis_hbm, out,
    spectra, dtheta, dphi, analysis, send, x, states, sums, got, edges, right, carries,
    load_sem, send_sem, recv_sem, back_send, back_recv, edge_send, edge_recv,
):
    loads = [
        pltpu.make_async_copy(source, target, load_sem.at[i])
        for i, (source, target) in enumerate(
            [(spectra_hbm, spectra), (dtheta_hbm, dtheta), (dphi_hbm, dphi), (analysis_hbm, analysis)]
        )
    ]
    for load in loads:
        load.start()
    greet([("ma", n), ("row", rows_count)])
    me = lax.axis_index("ma")
    row = lax.axis_index("row")
    slots = spectra.shape[3]
    points = spectra.shape[2]
    radii = RADII
    groups = points // radii
    halves = n // groups
    width = dtheta.shape[1] // halves
    chunks = width // 128
    orders = 2 * n
    keep = jnp.where(pair[me] == 0, 0.0, 1.0).astype(jnp.float32)
    lowest = pair[me]
    first, second, held, degree, order = slot_rows(lowest, slots)
    alive = held.astype(jnp.float32)
    l = degree.astype(jnp.float32)
    m = order.astype(jnp.float32)
    lower = jnp.sqrt((l * l - m * m) * alive / jnp.maximum(4.0 * l * l - 1.0, 1.0)) * ROTATION
    u = l + 1.0
    upper = jnp.sqrt(jnp.maximum((u * u - m * m) / (4.0 * u * u - 1.0), 0.0))
    upper = jnp.where(degree < LMAX, upper * alive, 0.0) * ROTATION
    spin = ROTATION * m / (l * (l + 1.0) + 2.0) * alive

    all_points = points * rows_count
    field = lax.broadcasted_iota(jnp.int32, (8, 1), 0) // 2
    nu = jnp.zeros((8, 1), jnp.float32)
    for f in range(4):
        nu = jnp.where(field == f, diffusivity[f], nu)
    off = nu * float((all_points + 1) ** 2)
    half_excess = (1.0 + nu * (l * (l + 1.0) / SHELL_RADIUS**2)) / (2.0 * off)
    root = jnp.sqrt(half_excess * half_excess + 2.0 * half_excess)
    inverse = 1.0 + half_excess + root
    rho = 1.0 / inverse
    log_rho = -jnp.log(inverse)
    inner = 1.0 / (2.0 * off * root)
    at = lax.broadcasted_iota(jnp.int32, (radii, slots), 0)
    near = (at + 1).astype(jnp.float32)
    far = (radii - at).astype(jnp.float32)

    def power(exponent):
        return jnp.exp(log_rho * exponent)

    for load in loads[:3]:
        load.wait()

    def block_for(e):
        group = e // halves
        half = lax.rem(e, halves)
        x = spectra[:, :, pl.ds(pl.multiple_of(group * radii, radii), radii), :]
        x = x.reshape(8 * radii, slots)
        lhs = jnp.concatenate([jnp.where(first, x, 0.0), jnp.where(second, x, 0.0)], axis=0)
        lhs = lhs.astype(jnp.bfloat16)
        columns = pl.ds(pl.multiple_of(half * width, 128), width)
        t = jnp.dot(lhs, dtheta[:, columns], preferred_element_type=jnp.float32)
        d = jnp.dot(lhs, dphi[:, columns], preferred_element_type=jnp.float32)
        t = t.reshape(2, 4, 2, radii, width)
        d = d.reshape(2, 4, 2, radii, width)
        parts = []
        for j in range(2):
            z_t, w_t, s_t, a_t = (t[j, f] for f in range(4))
            z_d, w_d, s_d, a_d = (d[j, f] for f in range(4))
            pieces = [
                (w_t[0] + z_d[1], w_t[1] - z_d[0]),
                (z_t[0] - w_d[1], z_t[1] + w_d[0]),
                (s_t[0], s_t[1]),
                (-s_d[1], s_d[0]),
                (a_d[1], -a_d[0]),
                (a_t[0], a_t[1]),
            ]
            for real, imag in pieces:
                parts += [real, imag * keep if j == 0 else imag]
        return jnp.concatenate(parts, axis=0).astype(jnp.bfloat16)

    def grid_copy(e, source, c):
        return pltpu.make_async_remote_copy(
            src_ref=send.at[c, e], dst_ref=x.at[c, source],
            send_sem=send_sem.at[c, e], recv_sem=recv_sem.at[c, source],
            device_id={"ma": e}, device_id_type=pl.DeviceIdType.MESH,
        )

    def back_copy(e, source, c):
        return pltpu.make_async_remote_copy(
            src_ref=sums.at[c, e], dst_ref=got.at[c, source],
            send_sem=back_send.at[c, e], recv_sem=back_recv.at[c, source],
            device_id={"ma": e}, device_id_type=pl.DeviceIdType.MESH,
        )

    target = ring(me, n)
    for step in far_first(n):
        e = target(*step)
        value = block_for(e)
        for c in range(chunks):
            send[c, e] = value[:, c * 128 : (c + 1) * 128]
        grid_copy(e, me, 0).start()
    for c in range(1, chunks):
        for step in far_first(n):
            grid_copy(target(*step), me, c).start()
    value = block_for(me)
    for c in range(chunks):
        x[c, me] = value[:, c * 128 : (c + 1) * 128]

    def couple(v):
        edge = jnp.zeros((points, 1), jnp.float32)
        below = jnp.concatenate([edge, v[:, : slots - 1]], axis=1)
        above = jnp.concatenate([v[:, 1:], edge], axis=1)
        return lower * below + upper * above

    z0, z1 = (jnp.where(held, spectra[0, c], 0.0) for c in range(2))
    w0, w1 = (jnp.where(held, spectra[1, c], 0.0) for c in range(2))
    right[0, 0] = z0 - spin * z1 + couple(w0) * alive
    right[0, 1] = z1 + spin * z0 + couple(w1) * alive
    right[1, 0] = w0 - spin * w1 - couple(z0) * alive
    right[1, 1] = w1 + spin * w0 - couple(z1) * alive
    for f in (2, 3):
        for c in range(2):
            right[f, c] = jnp.where(held, spectra[f, c], 0.0)

    zero = jnp.zeros((radii, 128), jnp.float32)
    for q in range(12):
        states[3 * orders, q] = zero

    def chunk_step(c, carry):
        def arrive(k, carry):
            e = lax.rem(me + k, n)
            grid_copy(e, e, c).wait_recv()
            return carry

        lax.fori_loop(1, n, arrive, 0)

        def unpack(g, carry):
            block = x[c, g].astype(jnp.float32).reshape(2, 6, 2, radii, 128)
            for j in range(2):
                at_order = 2 * g + j
                u_t, u_p, s_t, s_p, b_t, b_p = (block[j, q] for q in range(6))
                for q, (p, t) in enumerate(((b_p, b_t), (u_p, u_t), (s_p, s_t))):
                    plus = (p[0] - t[1], p[1] + t[0])
                    minus = (p[0] + t[1], p[1] - t[0])
                    parts = (plus[0], plus[1], minus[0], minus[1])
                    turned = (minus[0], -minus[1], plus[0], -plus[1])
                    for i in range(4):
                        states[at_order, 4 * q + i] = parts[i]
                        states[orders + at_order, 4 * q + i] = turned[i]
                        states[2 * orders + at_order, 4 * q + i] = 0.5 * parts[i]
            return carry

        lax.fori_loop(0, n, unpack, 0)

        def one_order(t, carry):
            def add(a, total):
                b = partner[t * orders + a]
                vp, vm, yp, ym, wp, wm = (
                    (states[a, 2 * q], states[a, 2 * q + 1], states[b, 2 * q], states[b, 2 * q + 1])
                    for q in range(6)
                )

                def square(v):
                    ar, ai, br, bi = v
                    return ar * br - ai * bi, ar * bi + ai * br

                def cross(v, w):
                    ar, ai, br, bi = v
                    cr, ci, dr, di = w
                    return (
                        (ar * dr - ai * di) + (cr * br - ci * bi),
                        (ar * di + ai * dr) + (cr * bi + ci * br),
                    )

                terms = []
                for v, y in ((vp, yp), (vm, ym)):
                    first_term, second_term = square(v), square(y)
                    terms += [first_term[0] - second_term[0], first_term[1] - second_term[1]]
                heat, other = cross(ym, wp), cross(yp, wm)
                terms += [heat[0] + other[0], heat[1] + other[1]]
                bent, other = cross(ym, vp), cross(yp, vm)
                terms += [bent[0] - other[0], bent[1] - other[1]]
                return tuple(v + w for v, w in zip(total, terms))

            pr, pi, mr, mi, hr, hi, er, ei = lax.fori_loop(0, orders, add, (zero,) * 8, unroll=4)
            rows = [pi - mi, mr - pr, pr + mr, pi + mi, -hr, -hi, ei, -er]
            rows = (0.5 * jnp.concatenate(rows, axis=0)).astype(jnp.bfloat16)
            sums[c, t // 2, pl.ds(pl.multiple_of(lax.rem(t, 2) * 8 * radii, 8 * radii), 8 * radii), :] = rows
            return carry

        lax.fori_loop(0, orders, one_order, 0)
        for step in far_first(n):
            back_copy(target(*step), me, c).start()
        got[c, me] = sums[c, me]
        return carry

    lax.fori_loop(0, chunks, chunk_step, 0)
    loads[3].wait()

    contract = (((1,), (1,)), ((), ()))
    own_group = me // halves
    for k in group_order(n, groups):
        g = lax.rem(own_group // k[2] + k[0], groups // k[2]) * k[2] + lax.rem(
            lax.rem(own_group, k[2]) + k[1], k[2]
        )
        rows = pl.ds(pl.multiple_of(g * radii, radii), radii)
        total = jnp.zeros((16 * radii, slots), jnp.float32)
        for h in range(halves):
            source = halves * g + h

            @pl.when(source != me)
            def _(source=source):
                for c in range(chunks):
                    back_copy(source, source, c).wait_recv()

            total += lax.dot_general(
                jnp.concatenate([got[c, source] for c in range(chunks)], axis=1),
                analysis[:, h * width : (h + 1) * width],
                contract, preferred_element_type=jnp.float32,
            )
        total = total.reshape(2, 4, 2, radii, slots)
        added = jnp.where(first, total[0], jnp.where(second, total[1], 0.0))
        last, start = [], []
        for f in range(4):
            scale = inner[2 * f : 2 * f + 1]
            for c in range(2):
                b = right[f, c, rows, :] + added[f, c]
                ahead, back = b, b
                ratio = rho[2 * f : 2 * f + 1]
                step = 1
                while step < radii:
                    ahead += ratio * jnp.where(at >= step, pltpu.roll(ahead, step, 0), 0.0)
                    back += ratio * jnp.where(
                        at < radii - step, pltpu.roll(back, radii - step, 0), 0.0
                    )
                    ratio = ratio * ratio
                    step *= 2
                right[f, c, rows, :] = scale * (ahead + back - b)
                last.append(ahead[radii - 1 : radii])
                start.append(back[0:1])
        carries[g, 0] = jnp.concatenate(last, axis=0)
        carries[g, 1] = jnp.concatenate(start, axis=0)

    hop = power(float(radii))
    ahead_at, back_at = [], []
    total = jnp.zeros((8, slots), jnp.float32)
    for g in range(groups):
        ahead_at.append(total)
        total = hop * total + carries[g, 0]
    edges[row, 0:8] = total
    total = jnp.zeros((8, slots), jnp.float32)
    for g in reversed(range(groups)):
        back_at.insert(0, total)
        total = hop * total + carries[g, 1]
    edges[row, 8:16] = total

    def edge_copy(e, source):
        return pltpu.make_async_remote_copy(
            src_ref=edges.at[row], dst_ref=edges.at[source],
            send_sem=edge_send.at[e], recv_sem=edge_recv.at[source],
            device_id={"row": e}, device_id_type=pl.DeviceIdType.MESH,
        )

    for k in range(1, rows_count):
        edge_copy(lax.rem(row + k, rows_count), row).start()

    before = (row * points).astype(jnp.float32)
    after = ((rows_count - 1 - row) * points).astype(jnp.float32)
    span = power(float(all_points + 1))
    scale = 1.0 / (1.0 - span * span)
    to_start, to_end = power(before), power(after)
    rise = [jnp.exp(log_rho[2 * f : 2 * f + 1] * near) for f in range(4)]
    fall = [jnp.exp(log_rho[2 * f : 2 * f + 1] * far) for f in range(4)]
    shifts = [power(float(k * points)) for k in range(rows_count)]
    inside = [power(float(k * radii)) for k in range(groups)]

    for c in range(chunks):
        for k in range(1, n):
            e = lax.rem(me + k, n)
            grid_copy(e, e, c).wait_send()
            back_copy(e, e, c).wait_send()
    for k in range(1, rows_count):
        e = lax.rem(row + k, rows_count)
        edge_copy(e, e).wait()

    zero = jnp.zeros((8, slots), jnp.float32)
    ahead_in, back_in, ahead_all, back_all = zero, zero, zero, zero
    for e in range(rows_count):
        f_e, g_e = edges[e, 0:8], edges[e, 8:16]
        weight, reverse = zero, zero
        for k in range(rows_count - 1):
            weight = jnp.where(row - 1 - e == k, shifts[k], weight)
            reverse = jnp.where(e - row - 1 == k, shifts[k], reverse)
        ahead_in += weight * f_e
        back_in += reverse * g_e
        ahead_all += shifts[rows_count - 1 - e] * f_e
        back_all += shifts[e] * g_e
    low = inner * rho * back_all
    high = inner * rho * ahead_all
    left = inner * ahead_in + (span * high - low) * scale * to_start
    rest = inner * back_in + (span * low - high) * scale * to_end
    for g in range(groups):
        here = left * inside[g] + inner * ahead_at[g]
        there = rest * inside[groups - 1 - g] + inner * back_at[g]
        for f in range(4):
            for c in range(2):
                i = 2 * f + c
                value = right[f, c, g * radii : (g + 1) * radii, :]
                value = value + here[i : i + 1] * rise[f] + there[i : i + 1] * fall[f]
                out[f, c, g * radii : (g + 1) * radii, :] = jnp.where(held, value, 0.0)


def group_order(n, groups):
    inner = 2 if groups % 2 == 0 and n == 2 * groups else 1
    steps = [(dy, dx, inner) for dy in range(groups // inner) for dx in range(inner)]
    return sorted(steps, key=lambda d: (d[0] > 0) + d[1])


def triad_table(pair_index):
    orders = jnp.stack([pair_index, LMAX - pair_index], axis=1).reshape(-1)
    count = orders.shape[0]
    need = orders[:, None] - orders[None, :]
    match = jnp.abs(need)[:, :, None] == orders[None, None, :]
    at = jnp.arange(count, dtype=jnp.int32)
    place = jnp.min(jnp.where(match, at, 3 * count), axis=2)
    place = jnp.where(jnp.logical_and(need < 0, place < count), place + count, place)
    place = jnp.where(need == orders[None, :], at[None, :] + 2 * count, place)
    return jnp.where(need > orders[None, :], 3 * count, place).reshape(-1)


def local(n, rows_count, spectra, dtheta, dphi, analysis, pair_index, diffusivity):
    points, slots = spectra.shape[2], spectra.shape[3]
    radii = RADII
    halves = n * radii // points
    width = -(-dtheta.shape[1] // (128 * halves)) * 128
    extra = width * halves - dtheta.shape[1]
    if extra:
        dtheta, dphi, analysis = (jnp.pad(v, ((0, 0), (0, extra))) for v in (dtheta, dphi, analysis))
    chunks = width // 128
    vmem = pl.BlockSpec(memory_space=pltpu.VMEM)
    smem = pl.BlockSpec(memory_space=pltpu.SMEM)
    hbm = pl.BlockSpec(memory_space=pltpu.HBM)
    shape = spectra.shape
    table = pltpu.VMEM(dtheta.shape, jnp.bfloat16)
    return pl.pallas_call(
        functools.partial(step_kernel, n, rows_count),
        out_shape=jax.ShapeDtypeStruct(shape, jnp.float32),
        in_specs=[smem, smem, smem, hbm, hbm, hbm, hbm],
        out_specs=vmem,
        scratch_shapes=[
            pltpu.VMEM(shape, jnp.float32),
            table,
            table,
            table,
            pltpu.VMEM((chunks, n, 24 * radii, 128), jnp.bfloat16),
            pltpu.VMEM((chunks, n, 24 * radii, 128), jnp.bfloat16),
            pltpu.VMEM((6 * n + 1, 12, radii, 128), jnp.float32),
            pltpu.VMEM((chunks, n, 16 * radii, 128), jnp.bfloat16),
            pltpu.VMEM((chunks, n, 16 * radii, 128), jnp.bfloat16),
            pltpu.VMEM((rows_count, 16, slots), jnp.float32),
            pltpu.VMEM(shape, jnp.float32),
            pltpu.VMEM((points // radii, 2, 8, slots), jnp.float32),
            pltpu.SemaphoreType.DMA((4,)),
            pltpu.SemaphoreType.DMA((chunks, n)),
            pltpu.SemaphoreType.DMA((chunks, n)),
            pltpu.SemaphoreType.DMA((chunks, n)),
            pltpu.SemaphoreType.DMA((chunks, n)),
            pltpu.SemaphoreType.DMA((rows_count,)),
            pltpu.SemaphoreType.DMA((rows_count,)),
        ],
        compiler_params=pltpu.CompilerParams(
            collective_id=0, has_side_effects=True, vmem_limit_bytes=VMEM_LIMIT
        ),
        name="step",
    )(triad_table(pair_index), pair_index, diffusivity, spectra, dtheta, dphi, analysis)


def solution(mesh):
    n, rows_count = mesh.shape["ma"], mesh.shape["row"]
    return jax.shard_map(
        functools.partial(local, n, rows_count),
        mesh=mesh,
        in_specs=(
            P(None, None, "row", "ma"),
            P("ma", None),
            P("ma", None),
            P("ma", None),
            P(),
            P(),
        ),
        out_specs=P(None, None, "row", "ma"),
        check_vma=False,
    )
```

time: 51.2 us -> 44.5 us (0.87)
  Pallas kernels: 45.8 us -> 40 us
  local copies, waits for them, and re-layouts: 4.88 us -> 3.19 us
  other arithmetic: 0 us -> 1.1 us
    pallas_call x3 -> x1, Pallas kernels: 45.8 us -> 40 us  [local(): pl.pallas_call(functools.partial(step_kernel, n, rows_count), out_shape=j...]
    unnamed x15 -> x3, local copies, waits for them, and re-layouts: 4.88 us -> 2.63 us
    select_n x0 -> x1, other arithmetic: none -> 0.58 us  [triad_table(): return jnp.where(need > orders[None, :], 3 * count, place).reshape(-1)]
where the time goes in v3:
time: 44.5 us; the launch traced here: 44.4 us
  Pallas kernels  40 us (90%)
  local copies, waits for them, and re-layouts  3.19 us (7%)
  other arithmetic  1.1 us (2%)
    pallas_call x1, Pallas kernels, local(): pl.pallas_call(functools.partial(step_kernel, n, rows_count), out_shape=j...  40 us
    unnamed x3, local copies, waits for them, and re-layouts  2.63 us

profile of v3, /device:TPU:0, one launch (start us, length us, event | category | flops | bytes accessed | tf_op | source)
XLA Modules:
  0.0 44.4 jit_solution(4194458615553914029)
XLA Ops:
  0.0 0.0 copy-start
  0.0 0.7 %copy-done = s32[8]{0:T(128)S(1)} copy-done((s32[8]{0:T(128)S(1)}, s32[8]{0:T(128)}, u32[]{:S(2)}) %copy-start) | copy-done | bytes 56
  0.7 0.1 copy.9
  0.8 0.1 sub.30
  0.8 0.1 broadcast_in_dim.26
  0.9 0.1 subtract_abs_fusion
  1.0 0.4 select_reduce_fusion
  1.4 0.1 reduce_min.12
  1.5 0.1 sub.34
  1.6 0.1 sub.31
  1.7 0.1 sub.32
  1.8 0.6 %compare_select_fusion.1.partner = s32[256]{0:T(256)} fusion(s32[256]{0:T(256)S(1)} %sub.34, s32[256]{0:T(256)S(1)} %broadcast_in_dim.26, s32[256]{0:T(256)S(1)} %reduce_min.12, s32[256]{0:T(256)S(1)} %sub.32), kind=kLoop, calls=%fused_computation.4 | loop fusion | flops 2560 | bytes 5120 | tf_op jit(solution)/shard_map/jit(_where)/select_n | solution.py:389
  2.3 40.0 %step.1 = f32[4,2,32,528]{3,2,1,0:T(8,128)} custom-call(s32[256]{0:T(256)} %compare_select_fusion.1.partner, s32[8]{0:T(128)} %pair.1, f32[4]{0:T(128)} %diffusivity.1, f32[4,2,32,528]{3,2,1,0:T(8,128)} %spectra_hbm.1, bf16[528,768]{1,0:T(8,128)(2,1)} %dtheta_hbm.1, bf16[528,768]{1,0:T(8,128)(2,1)} %dphi_hbm.1, bf16[528,768]{1,0:T(8,128)(2,1)} %analysis_hbm.1), custom_call_target="tpu_custom_call" | custom-call | tf_op jit(solution)/shard_map/step/pallas_call | solution.py:406
  42.4 2.0 %copy.11 = f32[4,2,32,528]{3,2,1,0:T(8,128)} copy(f32[4,2,32,528]{3,2,1,0:T(8,128)} %step.1) | data formatting | bytes 1081344
  (5 shorter events, 0.0 us)
Async XLA Ops:
  0.0 0.7 %copy-start = (s32[8]{0:T(128)S(1)}, s32[8]{0:T(128)}, u32[]{:S(2)}) copy-start(s32[8]{0:T(128)} %pair.1) | copy-start | bytes 100
